TPU v7x, 128 devices: a whole 4x4x4 slice. The times are simulated.
128 devices in a mesh: sec: 8 (over x_hi, z), tile: 16 (over y, x_lo, core).
Axes of the slice: x: 4 (x_hi: 2, x_lo: 2; x = x_hi * 2 + x_lo), y: 4, z: 4, core: 2. Of those that a mesh axis runs over, the one named last changes fastest.
Arguments:
- sections: float32 [8, 2048, 8192], P('sec', 'tile'), may hold values from -12 to 12
- masks: int32 [8, 32, 128], P('sec', 'tile'), may hold values 0 or 1
- carried: float32 [2, 32, 128], P(None, 'tile'), may hold values from -8 to 8
Outputs:
- flow: float32 [8, 2, 32, 128], P('sec', None, 'tile')
- aligned: float32 [8, 2, 32, 128], P('sec', None, 'tile')
All inputs are finite; a program needn't handle non-finite values. No bound on the sum of `masks` on one device may be relied on, other than what follows from the above.
Results may differ from a plain program's by a relative error of at most 0.000098.
Values sent between devices are 32-bit elements; how exact they have to be, the bound alone decides.
A program may use at most 128 MiB of HBM per device.

v0:
```python
import math

import jax
import jax.numpy as jnp
from jax import lax
from jax.sharding import PartitionSpec as P

COLS = 8192
PATCH = 128
STRIDE = 64
ITERS = 3


spring_weight = 1.0
link_weight = 4.0
anchor_weight = 0.5
highest = lax.Precision.HIGHEST


def passed_along(value, axis, steps):
    count = lax.axis_size(axis)
    initial, last = (max(0, -steps), min(count, count - steps))
    return lax.ppermute(value, axis, [(source, source + steps) for source in range(initial, last)])


def entering(part, axis, combine, identity):
    place = lax.axis_index(axis)
    gathered = lax.all_gather(part, axis)
    state = jnp.zeros_like(part) + jnp.asarray(identity, part.dtype)

    def one(lap, state):
        return combine(state, lax.dynamic_index_in_dim(gathered, lap, 0, False))

    return lax.fori_loop(0, place, one, state)


def with_halo(block, sides, width):
    for axis, dim in sides:
        count = lax.axis_size(axis)
        forward = [(i, i + 1) for i in range(count - 1)]
        backward = [(target, source) for source, target in forward]
        low = lax.ppermute(
            lax.slice_in_dim(block, block.shape[dim] - width, None, axis=dim), axis, forward
        )
        high = lax.ppermute(lax.slice_in_dim(block, 0, width, axis=dim), axis, backward)
        block = jnp.concatenate([low, block, high], axis=dim)
    return block


def tables():
    index = jnp.arange(PATCH, dtype=jnp.int32)
    phase = index[:, None] * index[None, :] % PATCH
    angle = phase.astype(jnp.float32) * (2.0 * math.pi / PATCH)
    return (jnp.cos(angle), jnp.sin(angle))


def shards(sections, masks, carried):
    node_rows = sections.shape[1] // STRIDE
    node_cols = COLS // STRIDE
    width = 16
    blocks = node_cols // width
    cosine, sine = tables()
    wrapped = ((jnp.arange(PATCH) + PATCH // 2) % PATCH - PATCH // 2).astype(jnp.float32)
    below = passed_along(sections[:, :STRIDE], "tile", -1)
    extended = jnp.concatenate([sections, below], axis=1)[0]
    extended = jnp.pad(extended, ((0, 0), (0, STRIDE)))

    def spectrum(image, first):
        window = lax.dynamic_slice_in_dim(image, first * STRIDE, (width + 1) * STRIDE, 1)
        cells = window.reshape(node_rows + 1, STRIDE, width + 1, STRIDE)
        row_pair = jnp.concatenate([cells[:-1], cells[1:]], axis=1)
        patches = jnp.concatenate([row_pair[:, :, :-1], row_pair[:, :, 1:]], axis=3)
        half_real = jnp.einsum("iyjx,xv->iyjv", patches, cosine, precision=highest)
        half_imag = -jnp.einsum("iyjx,xv->iyjv", patches, sine, precision=highest)
        full_real = jnp.einsum("uy,iyjv->iujv", cosine, half_real, precision=highest) + jnp.einsum(
            "uy,iyjv->iujv", sine, half_imag, precision=highest
        )
        full_imag = jnp.einsum("uy,iyjv->iujv", cosine, half_imag, precision=highest) - jnp.einsum(
            "uy,iyjv->iujv", sine, half_real, precision=highest
        )
        return jnp.stack([full_real, full_imag])

    def peaks(earlier, later):
        prod_real = earlier[0] * later[0] + earlier[1] * later[1]
        prod_imag = earlier[0] * later[1] - earlier[1] * later[0]
        back_real = jnp.einsum("iujv,vx->iujx", prod_real, cosine, precision=highest) - jnp.einsum(
            "iujv,vx->iujx", prod_imag, sine, precision=highest
        )
        back_imag = jnp.einsum("iujv,vx->iujx", prod_real, sine, precision=highest) + jnp.einsum(
            "iujv,vx->iujx", prod_imag, cosine, precision=highest
        )
        corr = (
            jnp.einsum("yu,iujx->iyjx", cosine, back_real, precision=highest)
            - jnp.einsum("yu,iujx->iyjx", sine, back_imag, precision=highest)
        ) / (PATCH * PATCH)
        scores = corr / PATCH
        top = jnp.max(scores, axis=(1, 3), keepdims=True)
        expo = jnp.exp(scores - top)
        total = jnp.sum(expo, axis=(1, 3))
        along_rows = jnp.sum(expo * wrapped[None, :, None, None], axis=(1, 3)) / total
        along_cols = jnp.sum(expo * wrapped[None, None, None, :], axis=(1, 3)) / total
        return jnp.stack([along_rows, along_cols])

    def earlier_of(own):
        return passed_along(own, ("sec", "tile"), lax.axis_size("tile"))

    def block_step(block, flow_acc):
        first = block * width
        own = spectrum(extended, first)
        part_flow = peaks(earlier_of(own), own)
        return lax.dynamic_update_slice_in_dim(flow_acc, part_flow, first, 2)

    flow = lax.fori_loop(0, blocks, block_step, jnp.zeros((2, node_rows, node_cols), jnp.float32))
    later_sec = (lax.axis_index("sec") > 0).astype(jnp.float32)
    flow = flow[None] * later_sec + carried[None] * (1.0 - later_sec)
    pairs = masks.astype(jnp.float32) * later_sec
    before = entering(flow, "sec", lambda early, late: early + late, jnp.zeros_like(flow))
    start = before + flow
    upcoming = passed_along(jnp.concatenate([flow, pairs[:, None]], axis=1), "sec", -1)
    next_flow = upcoming[:, :2]
    next_pair = upcoming[:, 2]
    rows = lax.axis_index("tile") * node_rows + jnp.arange(node_rows)
    total_rows = node_rows * lax.axis_size("tile")
    cols = jnp.arange(node_cols)
    degree = (
        4.0
        - (rows == 0).astype(jnp.float32)[:, None]
        - (rows == total_rows - 1).astype(jnp.float32)[:, None]
        - (cols == 0).astype(jnp.float32)[None, :]
        - (cols == node_cols - 1).astype(jnp.float32)[None, :]
    )
    denom = (
        spring_weight * degree[None] + link_weight * pairs + link_weight * next_pair + anchor_weight
    )
    aligned = start
    for step in range(ITERS):
        grown = with_halo(aligned, (("sec", 0), ("tile", 2)), 1)
        middle = grown[1:2]
        centre = middle[:, :, 1:-1]
        sideways = jnp.pad(centre, ((0, 0), (0, 0), (0, 0), (1, 1)))
        beside = (
            middle[:, :, :-2] + middle[:, :, 2:] + sideways[:, :, :, :-2] + sideways[:, :, :, 2:]
        )
        before = grown[0:1, :, 1:-1]
        after = grown[2:3, :, 1:-1]
        total = (
            spring_weight * beside
            + link_weight * pairs[:, None] * (before + flow)
            + link_weight * next_pair[:, None] * (after - next_flow)
            + anchor_weight * start
        )
        aligned = total / denom[:, None]
    return (flow, aligned)


def solution(mesh):
    in_specs = (P("sec", "tile", None), P("sec", "tile", None), P(None, "tile", None))
    out_specs = (P("sec", None, "tile", None), P("sec", None, "tile", None))
    return jax.shard_map(shards, mesh=mesh, in_specs=in_specs, out_specs=out_specs, check_vma=False)
```

profile of v0, /device:TPU:3, one launch (start us, length us, event | category | flops | bytes accessed | tf_op | source)
XLA Modules:
  0.0 1320.4 jit_solution(15047052793844768760)
XLA Ops:
  6.4 5.6 copy.31
  13.7 18.6 %collective-permute-done.1 = f32[1,64,8192]{2,1,0:T(8,128)S(1)} collective-permute-done((f32[1,64,8192]{2,1,0:T(8,128)}, f32[1,64,8192]{2,1,0:T(8,128)S(1)}, u32[]{:S(2)}, u32[]{:S(2)}) %collective-permute-start.1) | collective-permute-done | bytes 2097184 | tf_op jit(solution)/shard_map/ppermute | solution.py:23
  35.1 4.1 maximum_bitcast_fusion
  42.8 1182.5 %while.28 = (s32[]{:T(128)}, f32[2,2,128]{2,1,0:T(2,128)S(1)}, f32[192,8256]{0,1:T(8,128)}, s32[]{:T(128)}, s32[]{:T(128)}, /*index=5*/s32[]{:T(128)}, s32[]{:T(128)}, s32[]{}, s32[]{:T(128)}, s32[]{:T(128)}) while((s32[]{:T(128)}, f32[2,2,128]{2,1,0:T(2,128)S(1)}, f32[192,8256]{0,1:T(8,128)}, s32[]{:T(128)}, ...), condition=%wide.region_5.6_spmd.clone.clone, body=%wide.region_0.5_spmd.clone.clone.sunk | while | flops 9680848896 | bytes 118033960 | solution.py:113
  59.5 4.2 fusion.217
  70.0 5.5 collective-permute-start
  75.5 87.1 %collective-permute-done = f32[2,2,128,16,128]{2,4,3,1,0:T(8,128)} collective-permute-done((f32[2,2,128,16,128]{2,4,3,1,0:T(8,128)}, f32[2,2,128,16,128]{2,4,3,1,0:T(8,128)}, u32[]{:S(2)}, u32[]{:S(2)}) %collective-permute-start) | collective-permute-done | bytes 4194336 | tf_op jit(solution)/shard_map/while/body/eval_jaxpr/ppermute | solution.py:23
  216.3 5.8 collective-permute-start
  222.1 88.2 %collective-permute-done = f32[2,2,128,16,128]{2,4,3,1,0:T(8,128)} collective-permute-done((f32[2,2,128,16,128]{2,4,3,1,0:T(8,128)}, f32[2,2,128,16,128]{2,4,3,1,0:T(8,128)}, u32[]{:S(2)}, u32[]{:S(2)}) %collective-permute-start) | collective-permute-done | bytes 4194336 | tf_op jit(solution)/shard_map/while/body/eval_jaxpr/ppermute | solution.py:23
  324.9 4.0 fusion.225
  354.2 4.0 fusion.217
  364.5 5.8 collective-permute-start
  370.3 88.0 %collective-permute-done = f32[2,2,128,16,128]{2,4,3,1,0:T(8,128)} collective-permute-done((f32[2,2,128,16,128]{2,4,3,1,0:T(8,128)}, f32[2,2,128,16,128]{2,4,3,1,0:T(8,128)}, u32[]{:S(2)}, u32[]{:S(2)}) %collective-permute-start) | collective-permute-done | bytes 4194336 | tf_op jit(solution)/shard_map/while/body/eval_jaxpr/ppermute | solution.py:23
  512.2 6.1 collective-permute-start
  518.3 87.0 %collective-permute-done = f32[2,2,128,16,128]{2,4,3,1,0:T(8,128)} collective-permute-done((f32[2,2,128,16,128]{2,4,3,1,0:T(8,128)}, f32[2,2,128,16,128]{2,4,3,1,0:T(8,128)}, u32[]{:S(2)}, u32[]{:S(2)}) %collective-permute-start) | collective-permute-done | bytes 4194336 | tf_op jit(solution)/shard_map/while/body/eval_jaxpr/ppermute | solution.py:23
  619.9 4.0 fusion.225
  649.2 4.0 fusion.217
  659.5 7.6 collective-permute-start
  667.1 86.3 %collective-permute-done = f32[2,2,128,16,128]{2,4,3,1,0:T(8,128)} collective-permute-done((f32[2,2,128,16,128]{2,4,3,1,0:T(8,128)}, f32[2,2,128,16,128]{2,4,3,1,0:T(8,128)}, u32[]{:S(2)}, u32[]{:S(2)}) %collective-permute-start) | collective-permute-done | bytes 4194336 | tf_op jit(solution)/shard_map/while/body/eval_jaxpr/ppermute | solution.py:23
  807.4 8.8 collective-permute-start
  816.2 85.1 %collective-permute-done = f32[2,2,128,16,128]{2,4,3,1,0:T(8,128)} collective-permute-done((f32[2,2,128,16,128]{2,4,3,1,0:T(8,128)}, f32[2,2,128,16,128]{2,4,3,1,0:T(8,128)}, u32[]{:S(2)}, u32[]{:S(2)}) %collective-permute-start) | collective-permute-done | bytes 4194336 | tf_op jit(solution)/shard_map/while/body/eval_jaxpr/ppermute | solution.py:23
  945.2 4.0 fusion.217
  955.4 9.7 collective-permute-start
  965.2 84.2 %collective-permute-done = f32[2,2,128,16,128]{2,4,3,1,0:T(8,128)} collective-permute-done((f32[2,2,128,16,128]{2,4,3,1,0:T(8,128)}, f32[2,2,128,16,128]{2,4,3,1,0:T(8,128)}, u32[]{:S(2)}, u32[]{:S(2)}) %collective-permute-start) | collective-permute-done | bytes 4194336 | tf_op jit(solution)/shard_map/while/body/eval_jaxpr/ppermute | solution.py:23
  1103.4 9.7 collective-permute-start
  1113.1 83.2 %collective-permute-done = f32[2,2,128,16,128]{2,4,3,1,0:T(8,128)} collective-permute-done((f32[2,2,128,16,128]{2,4,3,1,0:T(8,128)}, f32[2,2,128,16,128]{2,4,3,1,0:T(8,128)}, u32[]{:S(2)}, u32[]{:S(2)}) %collective-permute-start) | collective-permute-done | bytes 4194336 | tf_op jit(solution)/shard_map/while/body/eval_jaxpr/ppermute | solution.py:23
  1225.4 40.0 %all-gather = f32[16,2,128]{2,1,0:T(2,128)S(1)} all-gather(f32[2,2,128]{2,1,0:T(2,128)S(1)} %multiply_add_fusion), channel_id=2, replica_groups=mesh['sec'=8,'tile'=16] {'sec'}, dimensions={0}, use_global_device_ids=true | all-gather | bytes 18432 | tf_op jit(solution)/shard_map/all_gather | solution.py:28
  1272.0 14.1 %collective-permute-start.5 = (f32[3,2,1,128]{3,2,1,0:T(1,128)S(1)}, f32[3,2,1,128]{3,2,1,0:T(1,128)S(1)}, u32[]{:S(2)}, u32[]{:S(2)}) collective-permute-start(f32[3,2,1,128]{3,2,1,0:T(1,128)S(1)} %get-tuple-element.297), channel_id=1, source_target_pairs={{1,0},{2,1},{3,2},{4,3},{5,4},{6,5},{7,6},{8,7},{9,8},{10,9},{11,1... | collective-permute-start | bytes 9224 | tf_op jit(solution)/shard_map/ppermute | solution.py:45
  1290.5 4.9 collective-permute-start.7
  1296.1 4.6 collective-permute-start.10
  1305.7 4.5 collective-permute-start.11
  1311.0 4.1 collective-permute-start.14
  (271 shorter events, 440.7 us)
Async XLA Ops:
  3.7 9.4 copy-start.2
  3.7 28.6 %collective-permute-start.1 = (f32[1,64,8192]{2,1,0:T(8,128)}, f32[1,64,8192]{2,1,0:T(8,128)S(1)}, u32[]{:S(2)}, u32[]{:S(2)}) collective-permute-start(f32[1,64,8192]{2,1,0:T(8,128)} %slice.155), channel_id=1, source_target_pairs={{1,0},{2,1},{3,2},{4,3},{5,4},{6,5},{7,6},{8,7},{9,8},{10,9},{11,1... | collective-permute-start | bytes 6291464 | tf_op jit(solution)/shard_map/ppermute | solution.py:23
  42.8 1182.6 %copy-start.5 = (f32[2,2,128]{2,1,0:T(2,128)S(1)}, f32[2,2,128]{2,1,0:T(2,128)}, u32[]{:S(2)}) copy-start(f32[2,2,128]{2,1,0:T(2,128)} %param.9) | copy-start | bytes 6148
  42.8 1227.8 %copy-start.4 = (f32[1,1,2,128]{3,2,1,0:T(2,128)S(1)}, f32[1,1,2,128]{3,2,1,0:T(2,128)}, u32[]{:S(2)}) copy-start(f32[1,1,2,128]{3,2,1,0:T(2,128)} %fusion.140) | copy-start | bytes 3076
  42.8 1245.2 %copy-start.3 = (s32[1,2,128]{2,1,0:T(2,128)S(1)}, s32[1,2,128]{2,1,0:T(2,128)}, u32[]{:S(2)}) copy-start(s32[1,2,128]{2,1,0:T(2,128)} %param.8) | copy-start | bytes 3076
  42.8 1245.2 %copy-start.6 = (f32[2]{0:T(128)S(1)}, f32[2]{0:T(128)}, u32[]{:S(2)}) copy-start(f32[2]{0:T(128)} %fusion.145) | copy-start | bytes 28
  42.8 1245.2 %copy-start.7 = (f32[128]{0:T(128)S(1)}, f32[128]{0:T(128)}, u32[]{:S(2)}) copy-start(f32[128]{0:T(128)} %get-tuple-element.300) | copy-start | bytes 1540
  42.8 1245.2 %copy-start.8 = (f32[128]{0:T(128)S(1)}, f32[128]{0:T(128)}, u32[]{:S(2)}) copy-start(f32[128]{0:T(128)} %get-tuple-element.301) | copy-start | bytes 1540
  67.4 2.6 copy-start
  70.0 92.7 %collective-permute-start = (f32[2,2,128,16,128]{2,4,3,1,0:T(8,128)}, f32[2,2,128,16,128]{2,4,3,1,0:T(8,128)}, u32[]{:S(2)}, u32[]{:S(2)}) collective-permute-start(f32[2,2,128,16,128]{2,4,3,1,0:T(8,128)} %pad_maximum_fusion.27), channel_id=1, source_target_pairs={{0,16},{1,17},{2,18},{3,19},{4,20},{5,21},{6,22},{7,23},{8,24},{9,... | collective-permute-start | bytes 12582920 | tf_op jit(solution)/shard_map/while/body/eval_jaxpr/ppermute | solution.py:23
  216.3 94.0 %collective-permute-start = (f32[2,2,128,16,128]{2,4,3,1,0:T(8,128)}, f32[2,2,128,16,128]{2,4,3,1,0:T(8,128)}, u32[]{:S(2)}, u32[]{:S(2)}) collective-permute-start(f32[2,2,128,16,128]{2,4,3,1,0:T(8,128)} %pad_maximum_fusion.27), channel_id=1, source_target_pairs={{0,16},{1,17},{2,18},{3,19},{4,20},{5,21},{6,22},{7,23},{8,24},{9,... | collective-permute-start | bytes 12582920 | tf_op jit(solution)/shard_map/while/body/eval_jaxpr/ppermute | solution.py:23
  364.5 93.8 %collective-permute-start = (f32[2,2,128,16,128]{2,4,3,1,0:T(8,128)}, f32[2,2,128,16,128]{2,4,3,1,0:T(8,128)}, u32[]{:S(2)}, u32[]{:S(2)}) collective-permute-start(f32[2,2,128,16,128]{2,4,3,1,0:T(8,128)} %pad_maximum_fusion.27), channel_id=1, source_target_pairs={{0,16},{1,17},{2,18},{3,19},{4,20},{5,21},{6,22},{7,23},{8,24},{9,... | collective-permute-start | bytes 12582920 | tf_op jit(solution)/shard_map/while/body/eval_jaxpr/ppermute | solution.py:23
  509.6 2.6 copy-start
  512.2 93.1 %collective-permute-start = (f32[2,2,128,16,128]{2,4,3,1,0:T(8,128)}, f32[2,2,128,16,128]{2,4,3,1,0:T(8,128)}, u32[]{:S(2)}, u32[]{:S(2)}) collective-permute-start(f32[2,2,128,16,128]{2,4,3,1,0:T(8,128)} %pad_maximum_fusion.27), channel_id=1, source_target_pairs={{0,16},{1,17},{2,18},{3,19},{4,20},{5,21},{6,22},{7,23},{8,24},{9,... | collective-permute-start | bytes 12582920 | tf_op jit(solution)/shard_map/while/body/eval_jaxpr/ppermute | solution.py:23
  659.5 93.9 %collective-permute-start = (f32[2,2,128,16,128]{2,4,3,1,0:T(8,128)}, f32[2,2,128,16,128]{2,4,3,1,0:T(8,128)}, u32[]{:S(2)}, u32[]{:S(2)}) collective-permute-start(f32[2,2,128,16,128]{2,4,3,1,0:T(8,128)} %pad_maximum_fusion.27), channel_id=1, source_target_pairs={{0,16},{1,17},{2,18},{3,19},{4,20},{5,21},{6,22},{7,23},{8,24},{9,... | collective-permute-start | bytes 12582920 | tf_op jit(solution)/shard_map/while/body/eval_jaxpr/ppermute | solution.py:23
  807.4 93.9 %collective-permute-start = (f32[2,2,128,16,128]{2,4,3,1,0:T(8,128)}, f32[2,2,128,16,128]{2,4,3,1,0:T(8,128)}, u32[]{:S(2)}, u32[]{:S(2)}) collective-permute-start(f32[2,2,128,16,128]{2,4,3,1,0:T(8,128)} %pad_maximum_fusion.27), channel_id=1, source_target_pairs={{0,16},{1,17},{2,18},{3,19},{4,20},{5,21},{6,22},{7,23},{8,24},{9,... | collective-permute-start | bytes 12582920 | tf_op jit(solution)/shard_map/while/body/eval_jaxpr/ppermute | solution.py:23
  955.4 93.9 %collective-permute-start = (f32[2,2,128,16,128]{2,4,3,1,0:T(8,128)}, f32[2,2,128,16,128]{2,4,3,1,0:T(8,128)}, u32[]{:S(2)}, u32[]{:S(2)}) collective-permute-start(f32[2,2,128,16,128]{2,4,3,1,0:T(8,128)} %pad_maximum_fusion.27), channel_id=1, source_target_pairs={{0,16},{1,17},{2,18},{3,19},{4,20},{5,21},{6,22},{7,23},{8,24},{9,... | collective-permute-start | bytes 12582920 | tf_op jit(solution)/shard_map/while/body/eval_jaxpr/ppermute | solution.py:23
  1103.4 93.0 %collective-permute-start = (f32[2,2,128,16,128]{2,4,3,1,0:T(8,128)}, f32[2,2,128,16,128]{2,4,3,1,0:T(8,128)}, u32[]{:S(2)}, u32[]{:S(2)}) collective-permute-start(f32[2,2,128,16,128]{2,4,3,1,0:T(8,128)} %pad_maximum_fusion.27), channel_id=1, source_target_pairs={{0,16},{1,17},{2,18},{3,19},{4,20},{5,21},{6,22},{7,23},{8,24},{9,... | collective-permute-start | bytes 12582920 | tf_op jit(solution)/shard_map/while/body/eval_jaxpr/ppermute | solution.py:23
  1225.3 94.9 %copy-start.1 = (f32[2,2,128]{2,1,0:T(2,128)}, f32[2,2,128]{2,1,0:T(2,128)S(1)}, u32[]{:S(2)}) copy-start(f32[2,2,128]{2,1,0:T(2,128)S(1)} %multiply_add_fusion) | copy-start | bytes 6148
  1265.3 6.6 collective-permute-start.3
  1266.6 5.3 collective-permute-start.2
  1270.6 17.4 %collective-permute-start.6 = (f32[1,3,2,128]{3,2,1,0:T(2,128)S(1)}, f32[1,3,2,128]{3,2,1,0:T(2,128)S(1)}, u32[]{:S(2)}, u32[]{:S(2)}) collective-permute-start(f32[1,3,2,128]{3,2,1,0:T(2,128)S(1)} %pad_maximum_fusion.6), channel_id=1, source_target_pairs={{16,0},{32,16},{48,32},{64,48},{80,64},{96,80},{112,96},{17,1},{33... | collective-permute-start | bytes 9224 | tf_op jit(solution)/shard_map/ppermute | solution.py:23
  1272.0 16.1 %collective-permute-start.5 = (f32[3,2,1,128]{3,2,1,0:T(1,128)S(1)}, f32[3,2,1,128]{3,2,1,0:T(1,128)S(1)}, u32[]{:S(2)}, u32[]{:S(2)}) collective-permute-start(f32[3,2,1,128]{3,2,1,0:T(1,128)S(1)} %get-tuple-element.297), channel_id=1, source_target_pairs={{1,0},{2,1},{3,2},{4,3},{5,4},{6,5},{7,6},{8,7},{9,8},{10,9},{11,1... | collective-permute-start | bytes 9224 | tf_op jit(solution)/shard_map/ppermute | solution.py:45
  1286.1 3.1 collective-permute-start.4
  1289.2 6.2 collective-permute-start.8
  1290.5 5.6 collective-permute-start.7
  1296.1 7.5 collective-permute-start.10
  1300.8 3.5 collective-permute-start.9
  1304.4 5.8 collective-permute-start.12
  1305.7 5.3 collective-permute-start.11
  1311.0 7.9 collective-permute-start.14
  1315.1 4.4 collective-permute-start.13
  (6 other events, 15.5 us)
where the time goes:
time: 1340 us; the launch traced here: 1320 us
  waiting for transfers between devices  712 us (53%)
  matrix products  311 us (23%)
  starting transfers between devices  112 us (8%)
  local copies, waits for them, and re-layouts  76.1 us (6%)
  other arithmetic  63.8 us (5%)
  blocking collectives  40 us (3%)
    ppermute x10, waiting for transfers between devices, passed_along(): lax.ppermute(value, axis, [(source, source + steps) for source in range(i...  708 us
    ppermute x10, starting transfers between devices, passed_along(): lax.ppermute(value, axis, [(source, source + steps) for source in range(i...  63 us
    slice x40, local copies, waits for them, and re-layouts, spectrum(): row_pair = jnp.concatenate([cells[:-1], cells[1:]], axis=1)  56.6 us
    all_gather x1, blocking collectives, entering(): gathered = lax.all_gather(part, axis)  40 us
    dot_general x8, matrix products, spectrum(): jnp.einsum('uy,iyjv->iujv', cosine, half_imag, precision=highest)  31.6 us
    dot_general x8, matrix products, peaks(): jnp.einsum('iujv,vx->iujx', prod_imag, sine, precision=highest)  31 us
    dot_general x8, matrix products, peaks(): jnp.einsum('yu,iujx->iyjx', cosine, back_real, precision=highest)  30.2 us
    sub x8, other arithmetic, peaks(): prod_imag = earlier[0] * later[1] - earlier[1] * later[0]  29.7 us
  transfers between devices with their start and end apart: 22, of which 14 were waited for; matrix products, arithmetic and copies ran while one was open for 1% of the time, Pallas kernels for 0%

commit v1 on v0

v1 whole, which is shorter than its diff:
```python
import functools
import math

import jax
import jax.numpy as jnp
import ml_dtypes
import numpy as np
from jax import lax
from jax.experimental import pallas as pl
from jax.experimental.pallas import tpu as pltpu
from jax.sharding import PartitionSpec as P

COLS = 8192
PATCH = 128
STRIDE = 64
ITERS = 3
HALF = PATCH // 2
TILES = 8
QUAD = 4
SIDE = 33

spring_weight = 1.0
link_weight = 4.0
anchor_weight = 0.5
bf16 = jnp.bfloat16
f32 = jnp.float32


def two_terms(table):
    table = table.astype(np.float32)
    high = table.astype(ml_dtypes.bfloat16)
    low = (table - high.astype(np.float32)).astype(ml_dtypes.bfloat16)
    return high, low


def tables():
    index = np.arange(PATCH)
    phase = np.outer(index, index) % PATCH
    cosine = np.cos(2 * np.pi * phase / PATCH)
    sine = np.sin(2 * np.pi * phase / PATCH)
    down = np.zeros((PATCH + 16, PATCH))
    down[:HALF] = cosine[:HALF]
    down[HALF:PATCH] = sine[:HALF]
    down[PATCH:] = cosine[HALF]
    high, low = two_terms(down)
    down = np.concatenate([high, high, low], 1)
    high, low = two_terms(np.block([[cosine, -sine], [-sine, -cosine]]))
    across = np.concatenate([high, high, low], 0)
    high, low = two_terms(np.block([[cosine, sine], [-sine, cosine]]))
    back = np.concatenate([high, high, low], 0)
    share = np.full(HALF, 2.0)
    share[0] = 1.0
    up = np.concatenate([cosine[:, :HALF] * share, -sine[:, :HALF] * share], 1)
    up[:, HALF] = cosine[:, HALF]
    high, low = two_terms(up * (math.log2(math.e) / PATCH**3))
    up = np.concatenate([high, high, low], 1)
    return down, across, back, up


def passed_along(value, axis, steps):
    count = lax.axis_size(axis)
    initial, last = (max(0, -steps), min(count, count - steps))
    return lax.ppermute(value, axis, [(source, source + steps) for source in range(initial, last)])


def split(value):
    high = value.astype(bf16)
    return high, (value - high.astype(f32)).astype(bf16)


def dot(left, right):
    return lax.dot_general(left, right, (((1,), (0,)), ((), ())), preferred_element_type=f32)


def three(value, axis):
    high, low = split(value)
    return jnp.concatenate([high, low, high], axis)


def cross(spec, count):
    ar, ai = spec[:count, :PATCH], spec[:count, PATCH:]
    br, bi = spec[count:, :PATCH], spec[count:, PATCH:]
    return three(jnp.concatenate([ar * br + ai * bi, ar * bi - ai * br], 1), 1)


def flow_chunk(loads, base, down, across, back, up, u_high, u_low, u_edge, g_edge, stat):
    for s in range(2):
        for tile in range(0, TILES + 1, 2):
            n = min(2, TILES + 1 - tile)
            top, mid, halo = [split(cell) for cell in loads[s](tile, n)]
            for r, first in ((0, top), (1, halo)):
                right = jnp.concatenate([first[0], mid[0], first[1], mid[1], first[0], mid[0]], 0)
                u = dot(down[...], right)
                high, low = split(u[:PATCH])
                lanes = slice(tile * 128, (tile + n) * 128)
                u_high[s, r, :, lanes] = high
                u_low[s, r, :, lanes] = low
                u_edge[s, r, :, lanes] = u[PATCH : PATCH + 8]
    left_lanes = lax.broadcasted_iota(jnp.int32, (HALF, 128), 1) < HALF
    left_lanes8 = lax.broadcasted_iota(jnp.int32, (8, 128), 1) < HALF
    sub8 = lax.broadcasted_iota(jnp.int32, (8, 128), 0)
    count = TILES * 4
    blocks = []
    for s in range(2):
        for group in range(count // 8):
            rows = jnp.zeros((8, 128), f32)
            for k in range(8):
                p = group * 8 + k
                tile, parity, r = p // 4, (p // 2) % 2, p % 2
                window = u_edge[s, r, :, tile * 128 : (tile + 1) * 128]
                if parity:
                    window = jnp.where(left_lanes8, u_edge[s, r, :, (tile + 1) * 128 : (tile + 2) * 128], window)
                rows = jnp.where(sub8 == k, window, rows)
            blocks.append(rows)
    real_rows = jnp.concatenate([across[i * 256 : i * 256 + 128] for i in range(3)], 0)
    spec = dot(three(jnp.concatenate(blocks, 0), 1), real_rows)
    g_edge[...] = dot(cross(spec, count), back[...])[:, :128]

    def some(i, carry):
        left = []
        for s in range(2):
            for q in range(QUAD):
                lane = pl.multiple_of((i * QUAD + q) * 128, 128)
                for parity in range(2):
                    for r in range(2):
                        parts = []
                        for ref in (u_high, u_low):
                            for half in range(2):
                                rows = slice(half * HALF, (half + 1) * HALF)
                                window = ref[s, r, rows, pl.ds(lane, 128)]
                                if parity:
                                    window = jnp.where(left_lanes, ref[s, r, rows, pl.ds(lane + 128, 128)], window)
                                parts.append(window)
                        left.append(jnp.concatenate(parts + parts[:2], 1))
        spec = dot(jnp.concatenate(left, 0), across[...])
        g = dot(cross(spec, QUAD * 4 * HALF), back[...])
        for j in range(QUAD * 2):
            columns = []
            for r in range(2):
                p = j * 2 + r
                real = g[p * HALF : (p + 1) * HALF, :128]
                imag = g[p * HALF : (p + 1) * HALF, 128:]
                edge = g_edge[pl.ds(i * QUAD * 4 + p, 1), :]
                first = jnp.where(sub8 == 0, jnp.broadcast_to(edge, (8, 128)), imag[:8])
                columns.append(jnp.concatenate([real, first, imag[8:]], 0))
            scores = dot(up[...], three(jnp.concatenate(columns, 1), 0))
            for r in range(2):
                part = [scores[k * 8 : (k + 1) * 8, r * 128 : (r + 1) * 128] for k in range(16)]
                tops = part
                while len(tops) > 1:
                    tops = [jnp.maximum(tops[2 * z], tops[2 * z + 1]) for z in range(len(tops) // 2)]
                expo = [jnp.exp2(k - tops[0]) for k in part]
                plus, plus_rows = expo[7], expo[7]
                for k in range(6, 0, -1):
                    plus = plus + expo[k]
                    plus_rows = plus_rows + plus
                plus = plus + expo[0]
                minus, minus_rows = expo[8], expo[8]
                for k in range(9, 16):
                    minus = minus + expo[k]
                    minus_rows = minus_rows + minus
                at = base + r * HALF + i * QUAD * 2 + j
                stat[0, pl.ds(at, 1)] = tops[0][None]
                stat[1, pl.ds(at, 1)] = (plus + minus)[None]
                stat[2, pl.ds(at, 1)] = (plus_rows - minus_rows)[None]
        return carry

    lax.fori_loop(0, TILES // QUAD, some, 0)


def flow_rows(stat, at, half):
    top, total, rows = (stat[k, pl.ds(at, HALF)] for k in range(3))
    most = jnp.max(jnp.max(top, axis=1, keepdims=True), axis=2, keepdims=True)
    scale = jnp.exp2(top - most)
    sub = lax.broadcasted_iota(jnp.int32, (1, 8, 128), 1).astype(f32)
    total = total * scale
    rows = jnp.sum(rows * scale * 8.0 + total * sub, axis=1)
    total = jnp.sum(total, axis=1)
    lane = lax.broadcasted_iota(jnp.int32, (HALF, 128), 1)
    wrapped = jnp.where(lane >= HALF, lane - PATCH, lane).astype(f32)
    columns = jnp.sum(total * wrapped, axis=1, keepdims=True)
    rows = jnp.sum(rows, axis=1, keepdims=True)
    total = jnp.sum(total, axis=1, keepdims=True)
    here = lane == lax.broadcasted_iota(jnp.int32, (HALF, 128), 0) + half * HALF
    return [
        jnp.sum(jnp.where(here, jnp.broadcast_to(v / total, (HALF, 128)), 0.0), axis=0, keepdims=True)
        for v in (rows, columns)
    ]


def flow_kernel(a, b, down, across, back, up, out, u_high, u_low, u_edge, g_edge, stat):
    chunks = (SIDE - 1) // TILES

    def one(c, carry):
        half = c // chunks
        first = half * SIDE + (c % chunks) * TILES

        def loader(ref):
            def load(tile, n):
                lane = pl.multiple_of((first + tile) * 128, 128)
                return [ref[z * HALF : (z + 1) * HALF, pl.ds(lane, n * 128)] for z in range(3)]

            return load

        base = half * 128 + (c % chunks) * TILES * 2
        flow_chunk([loader(a), loader(b)], base, down, across, back, up, u_high, u_low, u_edge, g_edge, stat)
        return carry

    lax.fori_loop(0, 2 * chunks, one, 0)
    for half in range(2):
        for r in range(2):
            for k, row in enumerate(flow_rows(stat, half * 128 + r * HALF, half)):
                out[half, k, pl.ds(r, 1), :] = row


def flow_of(a, b):
    vmem = pl.BlockSpec(memory_space=pltpu.VMEM)
    wide = (TILES + 1) * 128
    return pl.pallas_call(
        flow_kernel,
        out_shape=jax.ShapeDtypeStruct((2, 2, 2, 128), f32),
        in_specs=[vmem] * 6,
        out_specs=vmem,
        scratch_shapes=[
            pltpu.VMEM((2, 2, 128, wide), bf16),
            pltpu.VMEM((2, 2, 128, wide), bf16),
            pltpu.VMEM((2, 2, 8, wide), f32),
            pltpu.VMEM((TILES * 4, 128), f32),
            pltpu.VMEM((3, 256, 8, 128), f32),
        ],
        compiler_params=pltpu.CompilerParams(vmem_limit_bytes=56 << 20),
    )(a, b, *(jnp.asarray(t) for t in tables()))


def entering(part, axis, combine, identity):
    place = lax.axis_index(axis)
    gathered = lax.all_gather(part, axis)
    state = jnp.zeros_like(part) + jnp.asarray(identity, part.dtype)

    def one(lap, state):
        return combine(state, lax.dynamic_index_in_dim(gathered, lap, 0, False))

    return lax.fori_loop(0, place, one, state)


def with_halo(block, sides, width):
    for axis, dim in sides:
        count = lax.axis_size(axis)
        forward = [(i, i + 1) for i in range(count - 1)]
        backward = [(target, source) for source, target in forward]
        low = lax.ppermute(
            lax.slice_in_dim(block, block.shape[dim] - width, None, axis=dim), axis, forward
        )
        high = lax.ppermute(lax.slice_in_dim(block, 0, width, axis=dim), axis, backward)
        block = jnp.concatenate([low, block, high], axis=dim)
    return block


def shards(sections, masks, carried):
    node_rows = sections.shape[1] // STRIDE
    node_cols = COLS // STRIDE
    below = passed_along(sections[:, :STRIDE], "tile", -1)
    extended = jnp.concatenate([sections, below], axis=1)[0]
    extended = jnp.pad(extended, ((0, 0), (0, 128)))
    left = extended[:, : SIDE * 128]
    right = extended[:, COLS // 2 :]
    a = jnp.concatenate([passed_along(left, "sec", 1), right], 1)
    b = jnp.concatenate([left, passed_along(right, "sec", -1)], 1)
    pieces = flow_of(a, b)
    flow = pieces[0] + passed_along(pieces[1], "sec", 1)
    later_sec = (lax.axis_index("sec") > 0).astype(jnp.float32)
    flow = jnp.where(lax.axis_index("sec") > 0, flow, carried)[None]
    pairs = masks.astype(jnp.float32) * later_sec
    before = entering(flow, "sec", lambda early, late: early + late, jnp.zeros_like(flow))
    start = before + flow
    upcoming = passed_along(jnp.concatenate([flow, pairs[:, None]], axis=1), "sec", -1)
    next_flow = upcoming[:, :2]
    next_pair = upcoming[:, 2]
    rows = lax.axis_index("tile") * node_rows + jnp.arange(node_rows)
    total_rows = node_rows * lax.axis_size("tile")
    cols = jnp.arange(node_cols)
    degree = (
        4.0
        - (rows == 0).astype(jnp.float32)[:, None]
        - (rows == total_rows - 1).astype(jnp.float32)[:, None]
        - (cols == 0).astype(jnp.float32)[None, :]
        - (cols == node_cols - 1).astype(jnp.float32)[None, :]
    )
    denom = (
        spring_weight * degree[None] + link_weight * pairs + link_weight * next_pair + anchor_weight
    )
    aligned = start
    for step in range(ITERS):
        grown = with_halo(aligned, (("sec", 0), ("tile", 2)), 1)
        middle = grown[1:2]
        centre = middle[:, :, 1:-1]
        sideways = jnp.pad(centre, ((0, 0), (0, 0), (0, 0), (1, 1)))
        beside = (
            middle[:, :, :-2] + middle[:, :, 2:] + sideways[:, :, :, :-2] + sideways[:, :, :, 2:]
        )
        before = grown[0:1, :, 1:-1]
        after = grown[2:3, :, 1:-1]
        total = (
            spring_weight * beside
            + link_weight * pairs[:, None] * (before + flow)
            + link_weight * next_pair[:, None] * (after - next_flow)
            + anchor_weight * start
        )
        aligned = total / denom[:, None]
    return (flow, aligned)


def solution(mesh):
    in_specs = (P("sec", "tile", None), P("sec", "tile", None), P(None, "tile", None))
    out_specs = (P("sec", None, "tile", None), P("sec", None, "tile", None))
    return jax.shard_map(shards, mesh=mesh, in_specs=in_specs, out_specs=out_specs, check_vma=False)
```

time: 1340 us -> 292 us (0.22)
  the two profiles are of different devices: /device:TPU:3 before, /device:TPU:107 now
where the time goes in v1:
time: 292 us; the launch traced here: 291 us
  waiting for transfers between devices  116 us (40%)
  starting transfers between devices  67.9 us (23%)
  Pallas kernels  63.5 us (22%)
  blocking collectives  24.9 us (9%)
  other arithmetic  13.4 us (5%)
  local copies, waits for them, and re-layouts  4.84 us (2%)
    ppermute x5, waiting for transfers between devices, passed_along(): lax.ppermute(value, axis, [(source, source + steps) for source in range(i...  93.5 us
    pallas_call x1, Pallas kernels, flow_of(): pl.pallas_call(flow_kernel, out_shape=jax.ShapeDtypeStruct((2, 2, 2, 128)...  63.5 us
    ppermute x6, starting transfers between devices, with_halo(): lax.ppermute(lax.slice_in_dim(block, block.shape[dim] - width, None, axis...  39.7 us
    all_gather x1, blocking collectives, entering(): gathered = lax.all_gather(part, axis)  24.9 us
    ppermute x6, waiting for transfers between devices, with_halo(): lax.ppermute(lax.slice_in_dim(block, 0, width, axis=dim), axis, backward)  21.6 us
    ppermute x5, starting transfers between devices, passed_along(): lax.ppermute(value, axis, [(source, source + steps) for source in range(i...  16.7 us
    ppermute x6, starting transfers between devices, with_halo(): lax.ppermute(lax.slice_in_dim(block, 0, width, axis=dim), axis, backward)  11.5 us
    concatenate x1, other arithmetic, shards(): b = jnp.concatenate([left, passed_along(right, 'sec', -1)], 1)  6.02 us
  transfers between devices with their start and end apart: 17, of which 9 were waited for; matrix products, arithmetic and copies ran while one was open for 2% of the time, Pallas kernels for 0%

profile of v1, /device:TPU:107, one launch (start us, length us, event | category | flops | bytes accessed | tf_op | source)
XLA Modules:
  0.0 291.2 jit_solution(11705409868730508174)
XLA Ops:
  0.6 1.9 slice.100
  2.5 2.6 collective-permute-start
  5.1 25.7 %collective-permute-done = f32[1,64,8192]{2,1,0:T(8,128)S(1)} collective-permute-done((f32[1,64,8192]{2,1,0:T(8,128)S(1)}, f32[1,64,8192]{2,1,0:T(8,128)S(1)}, u32[]{:S(2)}, u32[]{:S(2)}) %collective-permute-start) | collective-permute-done | bytes 2097184 | tf_op jit(solution)/shard_map/ppermute | solution.py:63
  31.4 2.2 fusion.25
  33.6 2.0 collective-permute-start.2
  35.7 6.9 %collective-permute-start.1 = (f32[192,4224]{1,0:T(8,128)}, f32[192,4224]{1,0:T(8,128)}, u32[]{:S(2)}, u32[]{:S(2)}) collective-permute-start(f32[192,4224]{1,0:T(8,128)} %get-tuple-element.42), channel_id=1, source_target_pairs={{0,16},{16,32},{32,48},{48,64},{64,80},{80,96},{96,112},{1,17},{17... | collective-permute-start | bytes 9732104 | tf_op jit(solution)/shard_map/ppermute | solution.py:63
  42.6 66.9 %collective-permute-done.2 = f32[192,4224]{1,0:T(8,128)} collective-permute-done((f32[192,4224]{1,0:T(8,128)S(1)}, f32[192,4224]{1,0:T(8,128)}, u32[]{:S(2)}, u32[]{:S(2)}) %collective-permute-start.2) | collective-permute-done | bytes 3244064 | tf_op jit(solution)/shard_map/ppermute | solution.py:63
  109.5 6.0 %pad_maximum_fusion.1.b = f32[192,8448]{1,0:T(8,128)} fusion(f32[192,4224]{1,0:T(8,128)} %collective-permute-done.2, f32[192,4224]{1,0:T(8,128)} %get-tuple-element.42), kind=kLoop, calls=%fused_computation.2 | loop fusion | flops 1622016 | bytes 12976128 | tf_op jit(solution)/shard_map/concatenate | solution.py:268
  115.5 5.1 %pad_maximum_fusion.a = f32[192,8448]{1,0:T(8,128)} fusion(f32[192,4224]{1,0:T(8,128)S(1)} %get-tuple-element.43, f32[192,4224]{1,0:T(8,128)} %collective-permute-done.1), kind=kLoop, calls=%fused_computation.1 | loop fusion | flops 1622016 | bytes 12976128 | tf_op jit(solution)/shard_map/concatenate | solution.py:267
  120.6 63.5 %shard_map.86 = f32[2,2,2,128]{3,2,1,0:T(2,128)} custom-call(f32[192,8448]{1,0:T(8,128)} %pad_maximum_fusion.a, f32[192,8448]{1,0:T(8,128)} %pad_maximum_fusion.1.b, bf16[144,384]{1,0:T(8,128)(2,1)} %constant.45.clone.down, bf16[768,256]{1,0:T(8,128)(2,1)} %constant.46.clone.across, bf16[768,256]{1,0:T(8,128)(2,1)} %constant.47.clone.back, ...), custom_call_target="tpu_custom_call" | custom-call | tf_op jit(solution)/shard_map/pallas_call | solution.py:219
  184.8 3.4 %collective-permute-start.3 = (f32[2,2,128]{2,1,0:T(2,128)S(1)}, f32[2,2,128]{2,1,0:T(2,128)S(1)}, u32[]{:S(2)}, u32[]{:S(2)}) collective-permute-start(f32[2,2,128]{2,1,0:T(2,128)S(1)} %slice_bitcast_fusion), channel_id=1, source_target_pairs={{0,16},{16,32},{32,48},{48,64},{64,80},{80,96},{96,112},{1,17},{17... | collective-permute-start | bytes 6152 | tf_op jit(solution)/shard_map/ppermute | solution.py:63
  188.1 0.9 collective-permute-done.3
  189.8 24.9 %all-gather = f32[16,2,128]{2,1,0:T(2,128)S(1)} all-gather(f32[2,2,128]{2,1,0:T(2,128)S(1)} %fusion.16), channel_id=2, replica_groups=mesh['sec'=8,'tile'=16] {'sec'}, dimensions={0}, use_global_device_ids=true | all-gather | bytes 18432 | tf_op jit(solution)/shard_map/all_gather | solution.py:237
  214.7 7.3 %collective-permute-start.4 = (f32[1,2,2,128]{3,2,1,0:T(2,128)S(1)}, f32[1,2,2,128]{3,2,1,0:T(2,128)S(1)}, u32[]{:S(2)}, u32[]{:S(2)}) collective-permute-start(f32[1,2,2,128]{3,2,1,0:T(2,128)S(1)} %bitcast_add_fusion.2), channel_id=1, source_target_pairs={{0,16},{16,32},{32,48},{48,64},{64,80},{80,96},{96,112},{1,17},{17... | collective-permute-start | bytes 6152 | tf_op jit(solution)/shard_map/ppermute | solution.py:251
  222.0 1.9 collective-permute-start.5
  223.9 1.9 collective-permute-start.8
  225.9 4.1 %collective-permute-done.5 = f32[1,2,2,128]{3,2,1,0:T(2,128)S(1)} collective-permute-done((f32[1,2,2,128]{3,2,1,0:T(2,128)S(1)}, f32[1,2,2,128]{3,2,1,0:T(2,128)S(1)}, u32[]{:S(2)}, u32[]{:S(2)}) %collective-permute-start.5) | collective-permute-done | bytes 2080 | tf_op jit(solution)/shard_map/ppermute | solution.py:254
  229.9 11.4 %collective-permute-start.6 = (f32[3,2,1,128]{3,2,1,0:T(1,128)S(1)}, f32[3,2,1,128]{3,2,1,0:T(1,128)S(1)}, u32[]{:S(2)}, u32[]{:S(2)}) collective-permute-start(f32[3,2,1,128]{3,2,1,0:T(1,128)S(1)} %get-tuple-element.48), channel_id=1, source_target_pairs={{0,1},{1,2},{2,3},{3,4},{4,5},{5,6},{6,7},{7,8},{8,9},{9,10},{10,1... | collective-permute-start | bytes 9224 | tf_op jit(solution)/shard_map/ppermute | solution.py:251
  241.4 1.9 collective-permute-start.7
  243.4 3.8 %collective-permute-done.7 = f32[3,2,1,128]{3,2,1,0:T(1,128)S(1)} collective-permute-done((f32[3,2,1,128]{3,2,1,0:T(1,128)S(1)}, f32[3,2,1,128]{3,2,1,0:T(1,128)S(1)}, u32[]{:S(2)}, u32[]{:S(2)}) %collective-permute-start.7) | collective-permute-done | bytes 3104 | tf_op jit(solution)/shard_map/ppermute | solution.py:254
  247.3 1.9 collective-permute-start.10
  249.2 7.0 %collective-permute-start.9 = (f32[1,2,2,128]{3,2,1,0:T(2,128)S(1)}, f32[1,2,2,128]{3,2,1,0:T(2,128)S(1)}, u32[]{:S(2)}, u32[]{:S(2)}) collective-permute-start(f32[1,2,2,128]{3,2,1,0:T(2,128)S(1)} %add_divide_fusion.2), channel_id=1, source_target_pairs={{0,16},{16,32},{32,48},{48,64},{64,80},{80,96},{96,112},{1,17},{17... | collective-permute-start | bytes 6152 | tf_op jit(solution)/shard_map/ppermute | solution.py:251
  256.2 0.7 collective-permute-done.9
  256.9 3.1 %collective-permute-start.11 = (f32[3,2,1,128]{3,2,1,0:T(1,128)S(1)}, f32[3,2,1,128]{3,2,1,0:T(1,128)S(1)}, u32[]{:S(2)}, u32[]{:S(2)}) collective-permute-start(f32[3,2,1,128]{3,2,1,0:T(1,128)S(1)} %get-tuple-element.46), channel_id=1, source_target_pairs={{0,1},{1,2},{2,3},{3,4},{4,5},{5,6},{6,7},{7,8},{8,9},{9,10},{10,1... | collective-permute-start | bytes 9224 | tf_op jit(solution)/shard_map/ppermute | solution.py:251
  260.0 1.9 collective-permute-start.12
  261.9 3.9 %collective-permute-done.12 = f32[3,2,1,128]{3,2,1,0:T(1,128)S(1)} collective-permute-done((f32[3,2,1,128]{3,2,1,0:T(1,128)S(1)}, f32[3,2,1,128]{3,2,1,0:T(1,128)S(1)}, u32[]{:S(2)}, u32[]{:S(2)}) %collective-permute-start.12) | collective-permute-done | bytes 3104 | tf_op jit(solution)/shard_map/ppermute | solution.py:254
  265.9 6.9 %collective-permute-start.13 = (f32[1,2,2,128]{3,2,1,0:T(2,128)S(1)}, f32[1,2,2,128]{3,2,1,0:T(2,128)S(1)}, u32[]{:S(2)}, u32[]{:S(2)}) collective-permute-start(f32[1,2,2,128]{3,2,1,0:T(2,128)S(1)} %add_divide_fusion.1), channel_id=1, source_target_pairs={{0,16},{16,32},{32,48},{48,64},{64,80},{80,96},{96,112},{1,17},{17... | collective-permute-start | bytes 6152 | tf_op jit(solution)/shard_map/ppermute | solution.py:251
  272.8 1.9 collective-permute-start.14
  274.7 6.0 %collective-permute-done.14 = f32[1,2,2,128]{3,2,1,0:T(2,128)S(1)} collective-permute-done((f32[1,2,2,128]{3,2,1,0:T(2,128)S(1)}, f32[1,2,2,128]{3,2,1,0:T(2,128)S(1)}, u32[]{:S(2)}, u32[]{:S(2)}) %collective-permute-start.14) | collective-permute-done | bytes 2080 | tf_op jit(solution)/shard_map/ppermute | solution.py:254
  280.8 4.0 %collective-permute-start.15 = (f32[3,2,1,128]{3,2,1,0:T(1,128)S(1)}, f32[3,2,1,128]{3,2,1,0:T(1,128)S(1)}, u32[]{:S(2)}, u32[]{:S(2)}) collective-permute-start(f32[3,2,1,128]{3,2,1,0:T(1,128)S(1)} %get-tuple-element.44), channel_id=1, source_target_pairs={{0,1},{1,2},{2,3},{3,4},{4,5},{5,6},{6,7},{7,8},{8,9},{9,10},{10,1... | collective-permute-start | bytes 9224 | tf_op jit(solution)/shard_map/ppermute | solution.py:251
  284.8 1.9 collective-permute-start.16
  286.7 3.9 %collective-permute-done.16 = f32[3,2,1,128]{3,2,1,0:T(1,128)S(1)} collective-permute-done((f32[3,2,1,128]{3,2,1,0:T(1,128)S(1)}, f32[3,2,1,128]{3,2,1,0:T(1,128)S(1)}, u32[]{:S(2)}, u32[]{:S(2)}) %collective-permute-start.16) | collective-permute-done | bytes 3104 | tf_op jit(solution)/shard_map/ppermute | solution.py:254
  (40 shorter events, 3.1 us)
Async XLA Ops:
  0.6 30.2 %copy-start = (f32[1,128,8192]{2,1,0:T(8,128)S(1)}, f32[1,128,8192]{2,1,0:T(8,128)}, u32[]{:S(2)}) copy-start(f32[1,128,8192]{2,1,0:T(8,128)} %param.9) | copy-start | bytes 12582916
  2.5 28.3 %collective-permute-start = (f32[1,64,8192]{2,1,0:T(8,128)S(1)}, f32[1,64,8192]{2,1,0:T(8,128)S(1)}, u32[]{:S(2)}, u32[]{:S(2)}) collective-permute-start(f32[1,64,8192]{2,1,0:T(8,128)S(1)} %slice.100), channel_id=1, source_target_pairs={{1,0},{2,1},{3,2},{4,3},{5,4},{6,5},{7,6},{8,7},{9,8},{10,9},{11,1... | collective-permute-start | bytes 6291464 | tf_op jit(solution)/shard_map/ppermute | solution.py:63
  31.4 11.2 %copy-start.2 = (s32[1,2,128]{2,1,0:T(2,128)S(1)}, s32[1,2,128]{2,1,0:T(2,128)}, u32[]{:S(2)}) copy-start(s32[1,2,128]{2,1,0:T(2,128)} %param.10) | copy-start | bytes 3076
  33.6 75.9 %collective-permute-start.2 = (f32[192,4224]{1,0:T(8,128)S(1)}, f32[192,4224]{1,0:T(8,128)}, u32[]{:S(2)}, u32[]{:S(2)}) collective-permute-start(f32[192,4224]{1,0:T(8,128)S(1)} %get-tuple-element.43), channel_id=1, source_target_pairs={{16,0},{32,16},{48,32},{64,48},{80,64},{96,80},{112,96},{17,1},{33... | collective-permute-start | bytes 9732104 | tf_op jit(solution)/shard_map/ppermute | solution.py:63
  35.7 79.9 %collective-permute-start.1 = (f32[192,4224]{1,0:T(8,128)}, f32[192,4224]{1,0:T(8,128)}, u32[]{:S(2)}, u32[]{:S(2)}) collective-permute-start(f32[192,4224]{1,0:T(8,128)} %get-tuple-element.42), channel_id=1, source_target_pairs={{0,16},{16,32},{32,48},{48,64},{64,80},{80,96},{96,112},{1,17},{17... | collective-permute-start | bytes 9732104 | tf_op jit(solution)/shard_map/ppermute | solution.py:63
  120.6 68.5 %copy-start.3 = (f32[2,2,128]{2,1,0:T(2,128)S(1)}, f32[2,2,128]{2,1,0:T(2,128)}, u32[]{:S(2)}) copy-start(f32[2,2,128]{2,1,0:T(2,128)} %param.11) | copy-start | bytes 6148
  184.8 4.3 %collective-permute-start.3 = (f32[2,2,128]{2,1,0:T(2,128)S(1)}, f32[2,2,128]{2,1,0:T(2,128)S(1)}, u32[]{:S(2)}, u32[]{:S(2)}) collective-permute-start(f32[2,2,128]{2,1,0:T(2,128)S(1)} %slice_bitcast_fusion), channel_id=1, source_target_pairs={{0,16},{16,32},{32,48},{48,64},{64,80},{80,96},{96,112},{1,17},{17... | collective-permute-start | bytes 6152 | tf_op jit(solution)/shard_map/ppermute | solution.py:63
  189.8 101.5 %copy-start.1 = (f32[2,2,128]{2,1,0:T(2,128)}, f32[2,2,128]{2,1,0:T(2,128)S(1)}, u32[]{:S(2)}) copy-start(f32[2,2,128]{2,1,0:T(2,128)S(1)} %fusion.16) | copy-start | bytes 6148
  214.7 11.2 %collective-permute-start.4 = (f32[1,2,2,128]{3,2,1,0:T(2,128)S(1)}, f32[1,2,2,128]{3,2,1,0:T(2,128)S(1)}, u32[]{:S(2)}, u32[]{:S(2)}) collective-permute-start(f32[1,2,2,128]{3,2,1,0:T(2,128)S(1)} %bitcast_add_fusion.2), channel_id=1, source_target_pairs={{0,16},{16,32},{32,48},{48,64},{64,80},{80,96},{96,112},{1,17},{17... | collective-permute-start | bytes 6152 | tf_op jit(solution)/shard_map/ppermute | solution.py:251
  222.0 7.9 %collective-permute-start.5 = (f32[1,2,2,128]{3,2,1,0:T(2,128)S(1)}, f32[1,2,2,128]{3,2,1,0:T(2,128)S(1)}, u32[]{:S(2)}, u32[]{:S(2)}) collective-permute-start(f32[1,2,2,128]{3,2,1,0:T(2,128)S(1)} %bitcast_add_fusion.2), channel_id=1, source_target_pairs={{16,0},{32,16},{48,32},{64,48},{80,64},{96,80},{112,96},{17,1},{33... | collective-permute-start | bytes 6152 | tf_op jit(solution)/shard_map/ppermute | solution.py:254
  223.9 19.4 %collective-permute-start.8 = (f32[1,3,2,128]{3,2,1,0:T(2,128)S(1)}, f32[1,3,2,128]{3,2,1,0:T(2,128)S(1)}, u32[]{:S(2)}, u32[]{:S(2)}) collective-permute-start(f32[1,3,2,128]{3,2,1,0:T(2,128)S(1)} %pad_maximum_fusion.5), channel_id=1, source_target_pairs={{16,0},{32,16},{48,32},{64,48},{80,64},{96,80},{112,96},{17,1},{33... | collective-permute-start | bytes 9224 | tf_op jit(solution)/shard_map/ppermute | solution.py:63
  229.9 13.5 %collective-permute-start.6 = (f32[3,2,1,128]{3,2,1,0:T(1,128)S(1)}, f32[3,2,1,128]{3,2,1,0:T(1,128)S(1)}, u32[]{:S(2)}, u32[]{:S(2)}) collective-permute-start(f32[3,2,1,128]{3,2,1,0:T(1,128)S(1)} %get-tuple-element.48), channel_id=1, source_target_pairs={{0,1},{1,2},{2,3},{3,4},{4,5},{5,6},{6,7},{7,8},{8,9},{9,10},{10,1... | collective-permute-start | bytes 9224 | tf_op jit(solution)/shard_map/ppermute | solution.py:251
  241.4 5.8 %collective-permute-start.7 = (f32[3,2,1,128]{3,2,1,0:T(1,128)S(1)}, f32[3,2,1,128]{3,2,1,0:T(1,128)S(1)}, u32[]{:S(2)}, u32[]{:S(2)}) collective-permute-start(f32[3,2,1,128]{3,2,1,0:T(1,128)S(1)} %get-tuple-element.49), channel_id=1, source_target_pairs={{1,0},{2,1},{3,2},{4,3},{5,4},{6,5},{7,6},{8,7},{9,8},{10,9},{11,1... | collective-permute-start | bytes 9224 | tf_op jit(solution)/shard_map/ppermute | solution.py:254
  247.3 8.9 %collective-permute-start.10 = (f32[1,2,2,128]{3,2,1,0:T(2,128)S(1)}, f32[1,2,2,128]{3,2,1,0:T(2,128)S(1)}, u32[]{:S(2)}, u32[]{:S(2)}) collective-permute-start(f32[1,2,2,128]{3,2,1,0:T(2,128)S(1)} %add_divide_fusion.2), channel_id=1, source_target_pairs={{16,0},{32,16},{48,32},{64,48},{80,64},{96,80},{112,96},{17,1},{33... | collective-permute-start | bytes 6152 | tf_op jit(solution)/shard_map/ppermute | solution.py:254
  249.2 7.7 %collective-permute-start.9 = (f32[1,2,2,128]{3,2,1,0:T(2,128)S(1)}, f32[1,2,2,128]{3,2,1,0:T(2,128)S(1)}, u32[]{:S(2)}, u32[]{:S(2)}) collective-permute-start(f32[1,2,2,128]{3,2,1,0:T(2,128)S(1)} %add_divide_fusion.2), channel_id=1, source_target_pairs={{0,16},{16,32},{32,48},{48,64},{64,80},{80,96},{96,112},{1,17},{17... | collective-permute-start | bytes 6152 | tf_op jit(solution)/shard_map/ppermute | solution.py:251
  256.9 5.0 %collective-permute-start.11 = (f32[3,2,1,128]{3,2,1,0:T(1,128)S(1)}, f32[3,2,1,128]{3,2,1,0:T(1,128)S(1)}, u32[]{:S(2)}, u32[]{:S(2)}) collective-permute-start(f32[3,2,1,128]{3,2,1,0:T(1,128)S(1)} %get-tuple-element.46), channel_id=1, source_target_pairs={{0,1},{1,2},{2,3},{3,4},{4,5},{5,6},{6,7},{7,8},{8,9},{9,10},{10,1... | collective-permute-start | bytes 9224 | tf_op jit(solution)/shard_map/ppermute | solution.py:251
  260.0 5.8 %collective-permute-start.12 = (f32[3,2,1,128]{3,2,1,0:T(1,128)S(1)}, f32[3,2,1,128]{3,2,1,0:T(1,128)S(1)}, u32[]{:S(2)}, u32[]{:S(2)}) collective-permute-start(f32[3,2,1,128]{3,2,1,0:T(1,128)S(1)} %get-tuple-element.47), channel_id=1, source_target_pairs={{1,0},{2,1},{3,2},{4,3},{5,4},{6,5},{7,6},{8,7},{9,8},{10,9},{11,1... | collective-permute-start | bytes 9224 | tf_op jit(solution)/shard_map/ppermute | solution.py:254
  265.9 8.8 %collective-permute-start.13 = (f32[1,2,2,128]{3,2,1,0:T(2,128)S(1)}, f32[1,2,2,128]{3,2,1,0:T(2,128)S(1)}, u32[]{:S(2)}, u32[]{:S(2)}) collective-permute-start(f32[1,2,2,128]{3,2,1,0:T(2,128)S(1)} %add_divide_fusion.1), channel_id=1, source_target_pairs={{0,16},{16,32},{32,48},{48,64},{64,80},{80,96},{96,112},{1,17},{17... | collective-permute-start | bytes 6152 | tf_op jit(solution)/shard_map/ppermute | solution.py:251
  272.8 7.9 %collective-permute-start.14 = (f32[1,2,2,128]{3,2,1,0:T(2,128)S(1)}, f32[1,2,2,128]{3,2,1,0:T(2,128)S(1)}, u32[]{:S(2)}, u32[]{:S(2)}) collective-permute-start(f32[1,2,2,128]{3,2,1,0:T(2,128)S(1)} %add_divide_fusion.1), channel_id=1, source_target_pairs={{16,0},{32,16},{48,32},{64,48},{80,64},{96,80},{112,96},{17,1},{33... | collective-permute-start | bytes 6152 | tf_op jit(solution)/shard_map/ppermute | solution.py:254
  280.8 5.9 %collective-permute-start.15 = (f32[3,2,1,128]{3,2,1,0:T(1,128)S(1)}, f32[3,2,1,128]{3,2,1,0:T(1,128)S(1)}, u32[]{:S(2)}, u32[]{:S(2)}) collective-permute-start(f32[3,2,1,128]{3,2,1,0:T(1,128)S(1)} %get-tuple-element.44), channel_id=1, source_target_pairs={{0,1},{1,2},{2,3},{3,4},{4,5},{5,6},{6,7},{7,8},{8,9},{9,10},{10,1... | collective-permute-start | bytes 9224 | tf_op jit(solution)/shard_map/ppermute | solution.py:251
  284.8 5.8 %collective-permute-start.16 = (f32[3,2,1,128]{3,2,1,0:T(1,128)S(1)}, f32[3,2,1,128]{3,2,1,0:T(1,128)S(1)}, u32[]{:S(2)}, u32[]{:S(2)}) collective-permute-start(f32[3,2,1,128]{3,2,1,0:T(1,128)S(1)} %get-tuple-element.45), channel_id=1, source_target_pairs={{1,0},{2,1},{3,2},{4,3},{5,4},{6,5},{7,6},{8,7},{9,8},{10,9},{11,1... | collective-permute-start | bytes 9224 | tf_op jit(solution)/shard_map/ppermute | solution.py:254

commit v2 on v1

--- a/solution.py
+++ b/solution.py
@@ -1,4 +1,3 @@
-import functools
 import math
 
 import jax
@@ -18,6 +17,8 @@
 TILES = 8
 QUAD = 4
 SIDE = 33
+CHUNKS = 4
+MESH = pl.DeviceIdType.MESH
 
 spring_weight = 1.0
 link_weight = 4.0
@@ -55,12 +56,6 @@
     high, low = two_terms(up * (math.log2(math.e) / PATCH**3))
     up = np.concatenate([high, high, low], 1)
     return down, across, back, up
-
-
-def passed_along(value, axis, steps):
-    count = lax.axis_size(axis)
-    initial, last = (max(0, -steps), min(count, count - steps))
-    return lax.ppermute(value, axis, [(source, source + steps) for source in range(initial, last)])
 
 
 def split(value):
@@ -188,126 +183,367 @@
     ]
 
 
-def flow_kernel(a, b, down, across, back, up, out, u_high, u_low, u_edge, g_edge, stat):
-    chunks = (SIDE - 1) // TILES
-
-    def one(c, carry):
-        half = c // chunks
-        first = half * SIDE + (c % chunks) * TILES
-
-        def loader(ref):
-            def load(tile, n):
-                lane = pl.multiple_of((first + tile) * 128, 128)
-                return [ref[z * HALF : (z + 1) * HALF, pl.ds(lane, n * 128)] for z in range(3)]
-
-            return load
-
-        base = half * 128 + (c % chunks) * TILES * 2
-        flow_chunk([loader(a), loader(b)], base, down, across, back, up, u_high, u_low, u_edge, g_edge, stat)
+def flow_kernel(x, down, across, back, up, out, strips, u_high, u_low, u_edge, g_edge, stat,
+                own_sem, strip_send, strip_recv, halo_send, halo_recv, relay_send, relay_recv):
+    sec, tile = lax.axis_index("sec"), lax.axis_index("tile")
+    secs, tiles = lax.axis_size("sec"), lax.axis_size("tile")
+    barrier = pltpu.get_barrier_semaphore()
+    for place in (
+        (lax.rem(sec + 1, secs), tile),
+        (lax.rem(sec + secs - 1, secs), tile),
+        (sec, lax.rem(tile + 1, tiles)),
+        (sec, lax.rem(tile + tiles - 1, tiles)),
+    ):
+        pl.semaphore_signal(barrier, inc=1, device_id=place, device_id_type=MESH)
+    width = TILES * 128
+
+    def own(half):
+        first, n = (0, SIDE) if half == 0 else (SIDE - 1, SIDE - 1)
+        return pltpu.make_async_copy(
+            x.at[:, pl.ds(first * 128, n * 128)],
+            strips.at[1 - half, pl.ds(0, PATCH), pl.ds(half * SIDE * 128, n * 128)],
+            own_sem.at[half],
+        )
+
+    for half in range(2):
+        own(half).start()
+    pl.semaphore_wait(barrier, 4)
+
+    def spans(half, c, n):
+        source = pl.multiple_of((half * (SIDE - 1) + c * TILES) * 128, 128)
+        target = pl.multiple_of((half * SIDE + c * TILES) * 128, 128)
+        return pl.ds(source, n), pl.ds(target, n)
+
+    def strip(half, c, n=width):
+        source, target = spans(half, c, n)
+        return pltpu.make_async_remote_copy(
+            x.at[:, source],
+            strips.at[half, pl.ds(0, PATCH), target],
+            strip_send.at[half, c],
+            strip_recv.at[half, c],
+            device_id=(lax.rem(sec + 1 - 2 * half + secs, secs), tile),
+            device_id_type=MESH,
+        )
+
+    def halo(half, c, n=width):
+        source, target = spans(half, c, n)
+        return pltpu.make_async_remote_copy(
+            x.at[pl.ds(0, HALF), source],
+            strips.at[1 - half, pl.ds(PATCH, HALF), target],
+            halo_send.at[half, c],
+            halo_recv.at[half, c],
+            device_id=(sec, lax.rem(tile + tiles - 1, tiles)),
+            device_id_type=MESH,
+        )
+
+    def relay(half, c, n=width):
+        _, target = spans(half, c, n)
+        return pltpu.make_async_remote_copy(
+            strips.at[half, pl.ds(0, HALF), target],
+            strips.at[half, pl.ds(PATCH, HALF), target],
+            relay_send.at[half, c],
+            relay_recv.at[half, c],
+            device_id=(sec, lax.rem(tile + tiles - 1, tiles)),
+            device_id_type=MESH,
+        )
+
+    def gives(half):
+        return jnp.logical_or(jnp.logical_and(half == 0, sec < secs - 1), jnp.logical_and(half == 1, sec > 0))
+
+    def works(half):
+        return jnp.logical_or(jnp.logical_and(half == 0, sec > 0), jnp.logical_and(half == 1, sec < secs - 1))
+
+    above, under = tile > 0, tile < tiles - 1
+
+    def both(p, q):
+        return jnp.logical_and(p, q)
+
+    def step(i):
+        return lax.rem(i, 2), CHUNKS - 1 - i // 2
+
+    @pl.when(gives(0))
+    def _():
+        strip(0, CHUNKS, 128).start()
+
+    @pl.when(both(works(0), above))
+    def _():
+        halo(0, CHUNKS, 128).start()
+
+    def begin(i, carry):
+        half, c = step(i)
+
+        @pl.when(gives(half))
+        def _():
+            strip(half, c).start()
+
+        @pl.when(both(works(half), above))
+        def _():
+            halo(half, c).start()
+
         return carry
 
-    lax.fori_loop(0, 2 * chunks, one, 0)
+    lax.fori_loop(0, 2 * CHUNKS, begin, 0)
+    for s in range(2):
+        strips[s, :, (2 * SIDE - 1) * 128 :] = jnp.zeros((PATCH + HALF, 128), f32)
+
+    @pl.when(jnp.logical_not(under))
+    def _():
+        for s in range(2):
+            strips[s, PATCH:, : (2 * SIDE - 1) * 128] = jnp.zeros((HALF, (2 * SIDE - 1) * 128), f32)
+
+    for half in range(2):
+        own(half).wait()
+
+    @pl.when(works(0))
+    def _():
+        strip(0, CHUNKS, 128).wait_recv()
+
+        @pl.when(above)
+        def _():
+            relay(0, CHUNKS, 128).start()
+
+    def arrive(half, c):
+        @pl.when(works(half))
+        def _():
+            strip(half, c).wait_recv()
+
+            @pl.when(above)
+            def _():
+                relay(half, c).start()
+
+    arrive(*step(0))
+
+    @pl.when(both(works(0), under))
+    def _():
+        halo(0, CHUNKS, 128).wait_recv()
+        relay(0, CHUNKS, 128).wait_recv()
+
+    def one(i, carry):
+        half, c = step(i)
+
+        @pl.when(i + 1 < 2 * CHUNKS)
+        def _():
+            arrive(*step(i + 1))
+
+        @pl.when(works(half))
+        def _():
+            @pl.when(under)
+            def _():
+                halo(half, c).wait_recv()
+                relay(half, c).wait_recv()
+
+            def loader(s):
+                def load(tile, n):
+                    lane = pl.multiple_of((half * SIDE + c * TILES + tile) * 128, 128)
+                    return [strips[s, z * HALF : (z + 1) * HALF, pl.ds(lane, n * 128)] for z in range(3)]
+
+                return load
+
+            base = half * PATCH + c * TILES * 2
+            flow_chunk([loader(0), loader(1)], base, down, across, back, up, u_high, u_low, u_edge, g_edge, stat)
+
+        return carry
+
+    lax.fori_loop(0, 2 * CHUNKS, one, 0)
     for half in range(2):
         for r in range(2):
             for k, row in enumerate(flow_rows(stat, half * 128 + r * HALF, half)):
                 out[half, k, pl.ds(r, 1), :] = row
 
-
-def flow_of(a, b):
+    @pl.when(gives(0))
+    def _():
+        strip(0, CHUNKS, 128).wait_send()
+
+    @pl.when(both(works(0), above))
+    def _():
+        halo(0, CHUNKS, 128).wait_send()
+        relay(0, CHUNKS, 128).wait_send()
+
+    def end(i, carry):
+        half, c = step(i)
+
+        @pl.when(gives(half))
+        def _():
+            strip(half, c).wait_send()
+
+        @pl.when(both(works(half), above))
+        def _():
+            halo(half, c).wait_send()
+            relay(half, c).wait_send()
+
+        return carry
+
+    lax.fori_loop(0, 2 * CHUNKS, end, 0)
+
+
+def flow_of(x):
     vmem = pl.BlockSpec(memory_space=pltpu.VMEM)
     wide = (TILES + 1) * 128
+    dma = pltpu.SemaphoreType.DMA
     return pl.pallas_call(
         flow_kernel,
         out_shape=jax.ShapeDtypeStruct((2, 2, 2, 128), f32),
-        in_specs=[vmem] * 6,
+        in_specs=[pl.BlockSpec(memory_space=pl.ANY)] + [vmem] * 4,
         out_specs=vmem,
         scratch_shapes=[
+            pltpu.VMEM((2, PATCH + HALF, 2 * SIDE * 128), f32),
             pltpu.VMEM((2, 2, 128, wide), bf16),
             pltpu.VMEM((2, 2, 128, wide), bf16),
             pltpu.VMEM((2, 2, 8, wide), f32),
             pltpu.VMEM((TILES * 4, 128), f32),
             pltpu.VMEM((3, 256, 8, 128), f32),
-        ],
-        compiler_params=pltpu.CompilerParams(vmem_limit_bytes=56 << 20),
-    )(a, b, *(jnp.asarray(t) for t in tables()))
-
-
-def entering(part, axis, combine, identity):
-    place = lax.axis_index(axis)
-    gathered = lax.all_gather(part, axis)
-    state = jnp.zeros_like(part) + jnp.asarray(identity, part.dtype)
-
-    def one(lap, state):
-        return combine(state, lax.dynamic_index_in_dim(gathered, lap, 0, False))
-
-    return lax.fori_loop(0, place, one, state)
-
-
-def with_halo(block, sides, width):
-    for axis, dim in sides:
-        count = lax.axis_size(axis)
-        forward = [(i, i + 1) for i in range(count - 1)]
-        backward = [(target, source) for source, target in forward]
-        low = lax.ppermute(
-            lax.slice_in_dim(block, block.shape[dim] - width, None, axis=dim), axis, forward
+            dma((2,)),
+        ]
+        + [dma((2, CHUNKS + 1))] * 6,
+        compiler_params=pltpu.CompilerParams(vmem_limit_bytes=56 << 20, collective_id=0, has_side_effects=True),
+    )(x, *(jnp.asarray(t) for t in tables()))
+
+
+def relax_kernel(pieces, masks, carried, flow_out, aligned_out, blocks, result, sec_send, sec_recv, tile_send, tile_recv):
+    sec, tile = lax.axis_index("sec"), lax.axis_index("tile")
+    secs, tiles = lax.axis_size("sec"), lax.axis_size("tile")
+    barrier = pltpu.get_barrier_semaphore()
+    steps = (1, 2, tiles - 1, tiles - 2)
+    slots = (1, 0, 3, 4)
+    for k in range(1, secs):
+        pl.semaphore_signal(barrier, inc=1, device_id=(lax.rem(sec + k, secs), tile), device_id_type=MESH)
+    for k in steps:
+        pl.semaphore_signal(barrier, inc=1, device_id=(sec, lax.rem(tile + k, tiles)), device_id_type=MESH)
+    rows = [pieces[h, k] for h in range(2) for k in range(2)]
+    rows += [masks[...].astype(f32), carried[0], carried[1], jnp.zeros((2, 128), f32)]
+    blocks[2, pl.ds(sec, 1)] = jnp.concatenate(rows, 0)[None]
+    pl.semaphore_wait(barrier, secs - 1 + len(steps))
+
+    def to_sec(k, owner):
+        return pltpu.make_async_remote_copy(
+            blocks.at[2, owner],
+            blocks.at[2, owner],
+            sec_send.at[k],
+            sec_recv.at[k],
+            device_id=(lax.rem(sec + k, secs), tile),
+            device_id_type=MESH,
         )
-        high = lax.ppermute(lax.slice_in_dim(block, 0, width, axis=dim), axis, backward)
-        block = jnp.concatenate([low, block, high], axis=dim)
-    return block
-
-
-def shards(sections, masks, carried):
-    node_rows = sections.shape[1] // STRIDE
-    node_cols = COLS // STRIDE
-    below = passed_along(sections[:, :STRIDE], "tile", -1)
-    extended = jnp.concatenate([sections, below], axis=1)[0]
-    extended = jnp.pad(extended, ((0, 0), (0, 128)))
-    left = extended[:, : SIDE * 128]
-    right = extended[:, COLS // 2 :]
-    a = jnp.concatenate([passed_along(left, "sec", 1), right], 1)
-    b = jnp.concatenate([left, passed_along(right, "sec", -1)], 1)
-    pieces = flow_of(a, b)
-    flow = pieces[0] + passed_along(pieces[1], "sec", 1)
-    later_sec = (lax.axis_index("sec") > 0).astype(jnp.float32)
-    flow = jnp.where(lax.axis_index("sec") > 0, flow, carried)[None]
-    pairs = masks.astype(jnp.float32) * later_sec
-    before = entering(flow, "sec", lambda early, late: early + late, jnp.zeros_like(flow))
-    start = before + flow
-    upcoming = passed_along(jnp.concatenate([flow, pairs[:, None]], axis=1), "sec", -1)
-    next_flow = upcoming[:, :2]
-    next_pair = upcoming[:, 2]
-    rows = lax.axis_index("tile") * node_rows + jnp.arange(node_rows)
-    total_rows = node_rows * lax.axis_size("tile")
-    cols = jnp.arange(node_cols)
-    degree = (
-        4.0
-        - (rows == 0).astype(jnp.float32)[:, None]
-        - (rows == total_rows - 1).astype(jnp.float32)[:, None]
-        - (cols == 0).astype(jnp.float32)[None, :]
-        - (cols == node_cols - 1).astype(jnp.float32)[None, :]
-    )
-    denom = (
-        spring_weight * degree[None] + link_weight * pairs + link_weight * next_pair + anchor_weight
-    )
+
+    for k in range(1, secs):
+        to_sec(k, sec).start()
+    for k in range(1, secs):
+        to_sec(k, lax.rem(sec + secs - k, secs)).wait_recv()
+    copies = [
+        pltpu.make_async_remote_copy(
+            blocks.at[2],
+            blocks.at[slot],
+            tile_send.at[n],
+            tile_recv.at[n],
+            device_id=(sec, lax.rem(tile + k, tiles)),
+            device_id_type=MESH,
+        )
+        for n, (k, slot) in enumerate(zip(steps, slots))
+    ]
+    for copy in copies:
+        copy.start()
+    for copy in copies:
+        copy.wait_recv()
+
+    def window(get):
+        return jnp.concatenate([get(0)[1:2], get(1), get(2), get(3), get(4)[0:1]], 0)
+
+    flow = []
+    for s in range(secs):
+        if s == 0:
+            flow.append([window(lambda d: blocks[d, 0, 10 + 2 * k : 12 + 2 * k]) for k in range(2)])
+        else:
+            flow.append([
+                window(lambda d: blocks[d, s, 2 * k : 2 * k + 2] + blocks[d, s - 1, 4 + 2 * k : 6 + 2 * k])
+                for k in range(2)
+            ])
+    zero = jnp.zeros((8, 128), f32)
+    pairs = [zero] + [link_weight * window(lambda d: blocks[d, s, 8:10]) for s in range(1, secs)] + [zero]
+    node = 2 * tile - 3 + lax.broadcasted_iota(jnp.int32, (8, 128), 0)
+    column = lax.broadcasted_iota(jnp.int32, (8, 128), 1)
+    last = 2 * tiles - 1
+    inside = jnp.logical_and(node >= 0, node <= last)
+    at_left, at_right = column == 0, column == 127
+
+    def as_float(test):
+        return jnp.where(test, 1.0, 0.0)
+
+    degree = 4.0 - as_float(node == 0) - as_float(node == last) - as_float(at_left) - as_float(at_right)
+    start = [[jnp.where(inside, v, 0.0) for v in flow[0]]]
+    for s in range(1, secs):
+        start.append([start[s - 1][k] + jnp.where(inside, flow[s][k], 0.0) for k in range(2)])
+    inverse = [
+        jnp.where(inside, 1.0 / (spring_weight * degree + pairs[s] + pairs[s + 1] + anchor_weight), 0.0)
+        for s in range(secs)
+    ]
+    fixed = []
+    for s in range(secs):
+        row = []
+        for k in range(2):
+            v = anchor_weight * start[s][k]
+            if s > 0:
+                v = v + pairs[s] * flow[s][k]
+            if s + 1 < secs:
+                v = v - pairs[s + 1] * flow[s + 1][k]
+            row.append(v)
+        fixed.append(row)
     aligned = start
     for step in range(ITERS):
-        grown = with_halo(aligned, (("sec", 0), ("tile", 2)), 1)
-        middle = grown[1:2]
-        centre = middle[:, :, 1:-1]
-        sideways = jnp.pad(centre, ((0, 0), (0, 0), (0, 0), (1, 1)))
-        beside = (
-            middle[:, :, :-2] + middle[:, :, 2:] + sideways[:, :, :, :-2] + sideways[:, :, :, 2:]
-        )
-        before = grown[0:1, :, 1:-1]
-        after = grown[2:3, :, 1:-1]
-        total = (
-            spring_weight * beside
-            + link_weight * pairs[:, None] * (before + flow)
-            + link_weight * next_pair[:, None] * (after - next_flow)
-            + anchor_weight * start
-        )
-        aligned = total / denom[:, None]
-    return (flow, aligned)
+        new = []
+        for s in range(secs):
+            row = []
+            for k in range(2):
+                v = aligned[s][k]
+                total = fixed[s][k] + spring_weight * (
+                    pltpu.roll(v, 1, 0)
+                    + pltpu.roll(v, 7, 0)
+                    + jnp.where(at_left, 0.0, pltpu.roll(v, 1, 1))
+                    + jnp.where(at_right, 0.0, pltpu.roll(v, 127, 1))
+                )
+                if s > 0:
+                    total = total + pairs[s] * aligned[s - 1][k]
+                if s + 1 < secs:
+                    total = total + pairs[s + 1] * aligned[s + 1][k]
+                row.append(jnp.where(inside, total * inverse[s], 0.0))
+            new.append(row)
+        aligned = new
+    for s in range(secs):
+        for k in range(2):
+            result[s, k] = flow[s][k]
+            result[s, 2 + k] = aligned[s][k]
+    for k in range(2):
+        flow_out[k] = result[sec, k][3:5]
+        aligned_out[k] = result[sec, 2 + k][3:5]
+    for k in range(1, secs):
+        to_sec(k, sec).wait_send()
+    for copy in copies:
+        copy.wait_send()
+
+
+def relaxed(pieces, masks, carried):
+    vmem = pl.BlockSpec(memory_space=pltpu.VMEM)
+    dma = pltpu.SemaphoreType.DMA
+    secs = lax.axis_size("sec")
+    shape = jax.ShapeDtypeStruct((2, 2, 128), f32)
+    return pl.pallas_call(
+        relax_kernel,
+        out_shape=(shape, shape),
+        in_specs=[vmem] * 3,
+        out_specs=(vmem, vmem),
+        scratch_shapes=[
+            pltpu.VMEM((5, secs, 16, 128), f32),
+            pltpu.VMEM((secs, 4, 8, 128), f32),
+            dma((secs,)),
+            dma((secs,)),
+            dma((4,)),
+            dma((4,)),
+        ],
+        compiler_params=pltpu.CompilerParams(collective_id=1, has_side_effects=True),
+    )(pieces, masks, carried)
+
+
+def shards(sections, masks, carried):
+    flow, aligned = relaxed(flow_of(sections[0]), masks[0], carried)
+    return flow[None], aligned[None]
 
 
 def solution(mesh):

time: 292 us -> 157 us (0.54)
  the two profiles are of different devices: /device:TPU:107 before, /device:TPU:3 now
where the time goes in v2:
time: 157 us; the launch traced here: 156 us
  Pallas kernels  153 us (97%)
  local copies, waits for them, and re-layouts  2.48 us (2%)
    pallas_call x1, Pallas kernels, relaxed(): pl.pallas_call(relax_kernel, out_shape=(shape, shape), in_specs=[vmem] *...  86.8 us
    pallas_call x1, Pallas kernels, flow_of(): pl.pallas_call(flow_kernel, out_shape=jax.ShapeDtypeStruct((2, 2, 2, 128)...  66.2 us

profile of v2, /device:TPU:3, one launch (start us, length us, event | category | flops | bytes accessed | tf_op | source)
XLA Modules:
  0.0 156.1 jit_solution(18436250501621617092)
XLA Ops:
  0.6 66.2 %shard_map.86.pieces = f32[2,2,2,128]{3,2,1,0:T(2,128)} custom-call(f32[128,8192]{1,0:T(8,128)} %bitcast.4, bf16[144,384]{1,0:T(8,128)(2,1)} %constant.8.clone.down, bf16[768,256]{1,0:T(8,128)(2,1)} %constant.9.clone.across, bf16[768,256]{1,0:T(8,128)(2,1)} %constant.10.clone.back, bf16[128,384]{1,0:T(8,128)(2,1)} %constant.11.clone.up), custom_call_target="tpu_custom_call" | custom-call | tf_op jit(solution)/shard_map/pallas_call | solution.py:383
  66.8 86.8 %shard_map.87 = (f32[2,2,128]{2,1,0:T(2,128)}, f32[2,2,128]{2,1,0:T(2,128)}) custom-call(f32[2,2,2,128]{3,2,1,0:T(2,128)} %shard_map.86.pieces, s32[2,128]{1,0:T(2,128)} %bitcast.7, f32[2,2,128]{2,1,0:T(2,128)} %carried.1), custom_call_target="tpu_custom_call" | custom-call | tf_op jit(solution)/shard_map/pallas_call | solution.py:527
  153.7 1.2 copy.11
  154.9 1.2 copy.12

commit v3 on v2

--- a/solution.py
+++ b/solution.py
@@ -18,6 +18,7 @@
 QUAD = 4
 SIDE = 33
 CHUNKS = 4
+DETOUR = 3
 MESH = pl.DeviceIdType.MESH
 
 spring_weight = 1.0
@@ -195,6 +196,21 @@
         (sec, lax.rem(tile + tiles - 1, tiles)),
     ):
         pl.semaphore_signal(barrier, inc=1, device_id=place, device_id_type=MESH)
+    swapped = tile + 2 - 4 * lax.rem(tile // 2, 2)
+    first, last = sec == 0, sec == secs - 1
+    middle = secs // 2
+    lower, upper = sec == middle - 1, sec == middle
+
+    @pl.when(jnp.logical_or(first, last))
+    def _():
+        for there in (middle - 1, middle):
+            pl.semaphore_signal(barrier, inc=1, device_id=(there, swapped), device_id_type=MESH)
+
+    @pl.when(jnp.logical_or(lower, upper))
+    def _():
+        for there in (0, secs - 1):
+            pl.semaphore_signal(barrier, inc=1, device_id=(there, swapped), device_id_type=MESH)
+
     width = TILES * 128
 
     def own(half):
@@ -207,7 +223,8 @@
 
     for half in range(2):
         own(half).start()
-    pl.semaphore_wait(barrier, 4)
+    outer = jnp.logical_or(jnp.logical_or(first, last), jnp.logical_or(lower, upper))
+    pl.semaphore_wait(barrier, jnp.where(outer, 6, 4))
 
     def spans(half, c, n):
         source = pl.multiple_of((half * (SIDE - 1) + c * TILES) * 128, 128)
@@ -225,6 +242,38 @@
             device_id_type=MESH,
         )
 
+    def detour(half, c):
+        source, _ = spans(half, c, width)
+        _, target = spans(1 - half, c, width)
+        return pltpu.make_async_remote_copy(
+            x.at[:, source],
+            strips.at[1 - half, pl.ds(0, PATCH), target],
+            strip_send.at[half, c],
+            strip_recv.at[1 - half, c],
+            device_id=((secs - 1) * (1 - half), swapped),
+            device_id_type=MESH,
+        )
+
+    def onward(half, c):
+        _, source = spans(half, c, width)
+        _, target = spans(1 - half, c, width)
+        return pltpu.make_async_remote_copy(
+            strips.at[half, pl.ds(0, PATCH), source],
+            strips.at[1 - half, pl.ds(0, PATCH), target],
+            strip_send.at[1 - half, c],
+            strip_recv.at[1 - half, c],
+            device_id=(middle - 1 + half, swapped),
+            device_id_type=MESH,
+        )
+
+    def around(half, c):
+        mine = jnp.logical_or(jnp.logical_and(half == 0, lower), jnp.logical_and(half == 1, upper))
+        return jnp.logical_and(mine, c < DETOUR)
+
+    def passes(half, c):
+        mine = jnp.logical_or(jnp.logical_and(half == 0, first), jnp.logical_and(half == 1, last))
+        return jnp.logical_and(mine, c < DETOUR)
+
     def halo(half, c, n=width):
         source, target = spans(half, c, n)
         return pltpu.make_async_remote_copy(
@@ -272,9 +321,13 @@
     def begin(i, carry):
         half, c = step(i)
 
-        @pl.when(gives(half))
+        @pl.when(both(gives(half), jnp.logical_not(around(half, c))))
         def _():
             strip(half, c).start()
+
+        @pl.when(around(half, c))
+        def _():
+            detour(half, c).start()
 
         @pl.when(both(works(half), above))
         def _():
@@ -310,6 +363,11 @@
             @pl.when(above)
             def _():
                 relay(half, c).start()
+
+        @pl.when(passes(half, c))
+        def _():
+            detour(1 - half, c).wait_recv()
+            onward(half, c).start()
 
     arrive(*step(0))
 
@@ -362,9 +420,17 @@
     def end(i, carry):
         half, c = step(i)
 
-        @pl.when(gives(half))
+        @pl.when(both(gives(half), jnp.logical_not(around(half, c))))
         def _():
             strip(half, c).wait_send()
+
+        @pl.when(around(half, c))
+        def _():
+            detour(half, c).wait_send()
+
+        @pl.when(passes(half, c))
+        def _():
+            onward(half, c).wait_send()
 
         @pl.when(both(works(half), above))
         def _():

time: 157 us -> 124 us (0.79)
  Pallas kernels: 153 us -> 121 us
    pallas_call x1, Pallas kernels: 86.8 us -> 34.5 us  [relaxed(): pl.pallas_call(relax_kernel, out_shape=(shape, shape), in_specs=[vmem] *...]
    pallas_call x1, Pallas kernels: 66.2 us -> 86 us  [flow_of(): pl.pallas_call(flow_kernel, out_shape=jax.ShapeDtypeStruct((2, 2, 2, 128)...]
where the time goes in v3:
time: 124 us
  Pallas kernels  121 us (98%)
  local copies, waits for them, and re-layouts  2.48 us (2%)
    pallas_call x1, Pallas kernels, flow_of(): pl.pallas_call(flow_kernel, out_shape=jax.ShapeDtypeStruct((2, 2, 2, 128)...  86 us
    pallas_call x1, Pallas kernels, relaxed(): pl.pallas_call(relax_kernel, out_shape=(shape, shape), in_specs=[vmem] *...  34.5 us

profile of v3, /device:TPU:3, one launch (start us, length us, event | category | flops | bytes accessed | tf_op | source)
XLA Modules:
  0.0 123.7 jit_solution(1694120214006144813)
XLA Ops:
  0.6 86.0 %shard_map.86.pieces = f32[2,2,2,128]{3,2,1,0:T(2,128)} custom-call(f32[128,8192]{1,0:T(8,128)} %bitcast.4, bf16[144,384]{1,0:T(8,128)(2,1)} %constant.8.clone.down, bf16[768,256]{1,0:T(8,128)(2,1)} %constant.9.clone.across, bf16[768,256]{1,0:T(8,128)(2,1)} %constant.10.clone.back, bf16[128,384]{1,0:T(8,128)(2,1)} %constant.11.clone.up), custom_call_target="tpu_custom_call" | custom-call | tf_op jit(solution)/shard_map/pallas_call | solution.py:449
  86.7 34.5 %shard_map.87 = (f32[2,2,128]{2,1,0:T(2,128)}, f32[2,2,128]{2,1,0:T(2,128)}) custom-call(f32[2,2,2,128]{3,2,1,0:T(2,128)} %shard_map.86.pieces, s32[2,128]{1,0:T(2,128)} %bitcast.7, f32[2,2,128]{2,1,0:T(2,128)} %carried.1), custom_call_target="tpu_custom_call" | custom-call | tf_op jit(solution)/shard_map/pallas_call | solution.py:593
  121.2 1.2 copy.11
  122.4 1.2 %copy.12 = f32[1,2,2,128]{3,2,1,0:T(2,128)} copy(f32[1,2,2,128]{3,2,1,0:T(2,128)} %bitcast.5) | data formatting | bytes 4096

commit v4 on v3

--- a/solution.py
+++ b/solution.py
@@ -15,7 +15,7 @@
 ITERS = 3
 HALF = PATCH // 2
 TILES = 8
-QUAD = 4
+QUAD = 8
 SIDE = 33
 CHUNKS = 4
 DETOUR = 3
@@ -308,7 +308,9 @@
         return jnp.logical_and(p, q)
 
     def step(i):
-        return lax.rem(i, 2), CHUNKS - 1 - i // 2
+        apart = jnp.logical_or(lower, upper)
+        half = jnp.where(apart, lax.rem(i // CHUNKS + jnp.where(upper, 1, 0), 2), lax.rem(i, 2))
+        return half, CHUNKS - 1 - jnp.where(apart, lax.rem(i, CHUNKS), i // 2)
 
     @pl.when(gives(0))
     def _():

time: 124 us -> 119 us (0.960)
  Pallas kernels: 121 us -> 116 us
    pallas_call x1, Pallas kernels: 34.5 us -> 30.6 us  [relaxed(): pl.pallas_call(relax_kernel, out_shape=(shape, shape), in_specs=[vmem] *...]
where the time goes in v4:
time: 119 us
  Pallas kernels  116 us (97%)
  local copies, waits for them, and re-layouts  2.48 us (2%)
    pallas_call x1, Pallas kernels, flow_of(): pl.pallas_call(flow_kernel, out_shape=jax.ShapeDtypeStruct((2, 2, 2, 128)...  85.5 us
    pallas_call x1, Pallas kernels, relaxed(): pl.pallas_call(relax_kernel, out_shape=(shape, shape), in_specs=[vmem] *...  30.6 us
    unnamed x2, local copies, waits for them, and re-layouts  2.48 us

profile of v4, /device:TPU:3, one launch (start us, length us, event | category | flops | bytes accessed | tf_op | source)
XLA Modules:
  0.0 119.2 jit_solution(11654201558244797014)
XLA Ops:
  0.6 85.5 %shard_map.86.pieces = f32[2,2,2,128]{3,2,1,0:T(2,128)} custom-call(f32[128,8192]{1,0:T(8,128)} %bitcast.4, bf16[144,384]{1,0:T(8,128)(2,1)} %constant.8.clone.down, bf16[768,256]{1,0:T(8,128)(2,1)} %constant.9.clone.across, bf16[768,256]{1,0:T(8,128)(2,1)} %constant.10.clone.back, bf16[128,384]{1,0:T(8,128)(2,1)} %constant.11.clone.up), custom_call_target="tpu_custom_call" | custom-call | tf_op jit(solution)/shard_map/pallas_call | solution.py:451
  86.2 30.6 %shard_map.87 = (f32[2,2,128]{2,1,0:T(2,128)}, f32[2,2,128]{2,1,0:T(2,128)}) custom-call(f32[2,2,2,128]{3,2,1,0:T(2,128)} %shard_map.86.pieces, s32[2,128]{1,0:T(2,128)} %bitcast.7, f32[2,2,128]{2,1,0:T(2,128)} %carried.1), custom_call_target="tpu_custom_call" | custom-call | tf_op jit(solution)/shard_map/pallas_call | solution.py:595
  116.7 1.2 %copy.11 = f32[1,2,2,128]{3,2,1,0:T(2,128)} copy(f32[1,2,2,128]{3,2,1,0:T(2,128)} %bitcast.6) | data formatting | bytes 4096
  118.0 1.2 %copy.12 = f32[1,2,2,128]{3,2,1,0:T(2,128)} copy(f32[1,2,2,128]{3,2,1,0:T(2,128)} %bitcast.5) | data formatting | bytes 4096

commit v5 on v4

--- a/solution.py
+++ b/solution.py
@@ -79,7 +79,7 @@
     return three(jnp.concatenate([ar * br + ai * bi, ar * bi - ai * br], 1), 1)
 
 
-def flow_chunk(loads, base, down, across, back, up, u_high, u_low, u_edge, g_edge, stat):
+def flow_chunk(loads, base, down, across, back, up, u_high, u_low, u_edge, g_edge, stat, between):
     for s in range(2):
         for tile in range(0, TILES + 1, 2):
             n = min(2, TILES + 1 - tile)
@@ -111,6 +111,7 @@
     real_rows = jnp.concatenate([across[i * 256 : i * 256 + 128] for i in range(3)], 0)
     spec = dot(three(jnp.concatenate(blocks, 0), 1), real_rows)
     g_edge[...] = dot(cross(spec, count), back[...])[:, :128]
+    between()
 
     def some(i, carry):
         left = []
@@ -381,9 +382,12 @@
     def one(i, carry):
         half, c = step(i)
 
-        @pl.when(i + 1 < 2 * CHUNKS)
-        def _():
-            arrive(*step(i + 1))
+        def advance():
+            @pl.when(i + 1 < 2 * CHUNKS)
+            def _():
+                arrive(*step(i + 1))
+
+        pl.when(jnp.logical_not(works(half)))(advance)
 
         @pl.when(works(half))
         def _():
@@ -400,7 +404,7 @@
                 return load
 
             base = half * PATCH + c * TILES * 2
-            flow_chunk([loader(0), loader(1)], base, down, across, back, up, u_high, u_low, u_edge, g_edge, stat)
+            flow_chunk([loader(0), loader(1)], base, down, across, back, up, u_high, u_low, u_edge, g_edge, stat, advance)
 
         return carry
 
@@ -467,7 +471,7 @@
     )(x, *(jnp.asarray(t) for t in tables()))
 
 
-def relax_kernel(pieces, masks, carried, flow_out, aligned_out, blocks, result, sec_send, sec_recv, tile_send, tile_recv):
+def relax_kernel(pieces, masks, carried, flow_out, aligned_out, mine, blocks, result, sec_send, sec_recv, tile_send, tile_recv):
     sec, tile = lax.axis_index("sec"), lax.axis_index("tile")
     secs, tiles = lax.axis_size("sec"), lax.axis_size("tile")
     barrier = pltpu.get_barrier_semaphore()
@@ -479,13 +483,13 @@
         pl.semaphore_signal(barrier, inc=1, device_id=(sec, lax.rem(tile + k, tiles)), device_id_type=MESH)
     rows = [pieces[h, k] for h in range(2) for k in range(2)]
     rows += [masks[...].astype(f32), carried[0], carried[1], jnp.zeros((2, 128), f32)]
-    blocks[2, pl.ds(sec, 1)] = jnp.concatenate(rows, 0)[None]
+    mine[pl.ds(sec, 1)] = jnp.concatenate(rows, 0)[None]
     pl.semaphore_wait(barrier, secs - 1 + len(steps))
 
     def to_sec(k, owner):
         return pltpu.make_async_remote_copy(
-            blocks.at[2, owner],
-            blocks.at[2, owner],
+            mine.at[owner],
+            mine.at[owner],
             sec_send.at[k],
             sec_recv.at[k],
             device_id=(lax.rem(sec + k, secs), tile),
@@ -496,6 +500,9 @@
         to_sec(k, sec).start()
     for k in range(1, secs):
         to_sec(k, lax.rem(sec + secs - k, secs)).wait_recv()
+    for s in range(secs):
+        whole = mine[0, 10:14] if s == 0 else mine[s, 0:4] + mine[s - 1, 4:8]
+        blocks[2, s] = jnp.concatenate([whole, mine[s, 8:10], jnp.zeros((2, 128), f32)], 0)
     copies = [
         pltpu.make_async_remote_copy(
             blocks.at[2],
@@ -515,17 +522,9 @@
     def window(get):
         return jnp.concatenate([get(0)[1:2], get(1), get(2), get(3), get(4)[0:1]], 0)
 
-    flow = []
-    for s in range(secs):
-        if s == 0:
-            flow.append([window(lambda d: blocks[d, 0, 10 + 2 * k : 12 + 2 * k]) for k in range(2)])
-        else:
-            flow.append([
-                window(lambda d: blocks[d, s, 2 * k : 2 * k + 2] + blocks[d, s - 1, 4 + 2 * k : 6 + 2 * k])
-                for k in range(2)
-            ])
+    flow = [[window(lambda d: blocks[d, s, 2 * k : 2 * k + 2]) for k in range(2)] for s in range(secs)]
     zero = jnp.zeros((8, 128), f32)
-    pairs = [zero] + [link_weight * window(lambda d: blocks[d, s, 8:10]) for s in range(1, secs)] + [zero]
+    pairs = [zero] + [link_weight * window(lambda d: blocks[d, s, 4:6]) for s in range(1, secs)] + [zero]
     node = 2 * tile - 3 + lax.broadcasted_iota(jnp.int32, (8, 128), 0)
     column = lax.broadcasted_iota(jnp.int32, (8, 128), 1)
     last = 2 * tiles - 1
@@ -598,7 +597,8 @@
         in_specs=[vmem] * 3,
         out_specs=(vmem, vmem),
         scratch_shapes=[
-            pltpu.VMEM((5, secs, 16, 128), f32),
+            pltpu.VMEM((secs, 16, 128), f32),
+            pltpu.VMEM((5, secs, 8, 128), f32),
             pltpu.VMEM((secs, 4, 8, 128), f32),
             dma((secs,)),
             dma((secs,)),

time: 119 us -> 120 us (level); the launches traced: 119 us -> 119 us
  no operation moved by 1% of the time
where the time goes in v5:
time: 120 us; the launch traced here: 119 us
  Pallas kernels  116 us (97%)
  local copies, waits for them, and re-layouts  2.48 us (2%)
    pallas_call x1, Pallas kernels, flow_of(): pl.pallas_call(flow_kernel, out_shape=jax.ShapeDtypeStruct((2, 2, 2, 128)...  85.8 us
    pallas_call x1, Pallas kernels, relaxed(): pl.pallas_call(relax_kernel, out_shape=(shape, shape), in_specs=[vmem] *...  29.9 us
    unnamed x2, local copies, waits for them, and re-layouts  2.48 us

profile of v5, /device:TPU:3, one launch (start us, length us, event | category | flops | bytes accessed | tf_op | source)
XLA Modules:
  0.0 118.8 jit_solution(10358513303575879698)
XLA Ops:
  0.6 85.8 %shard_map.86.pieces = f32[2,2,2,128]{3,2,1,0:T(2,128)} custom-call(f32[128,8192]{1,0:T(8,128)} %bitcast.4, bf16[144,384]{1,0:T(8,128)(2,1)} %constant.8.clone.down, bf16[768,256]{1,0:T(8,128)(2,1)} %constant.9.clone.across, bf16[768,256]{1,0:T(8,128)(2,1)} %constant.10.clone.back, bf16[128,384]{1,0:T(8,128)(2,1)} %constant.11.clone.up), custom_call_target="tpu_custom_call" | custom-call | tf_op jit(solution)/shard_map/pallas_call | solution.py:455
  86.4 29.9 %shard_map.87 = (f32[2,2,128]{2,1,0:T(2,128)}, f32[2,2,128]{2,1,0:T(2,128)}) custom-call(f32[2,2,2,128]{3,2,1,0:T(2,128)} %shard_map.86.pieces, s32[2,128]{1,0:T(2,128)} %bitcast.7, f32[2,2,128]{2,1,0:T(2,128)} %carried.1), custom_call_target="tpu_custom_call" | custom-call | tf_op jit(solution)/shard_map/pallas_call | solution.py:594
  116.3 1.2 %copy.11 = f32[1,2,2,128]{3,2,1,0:T(2,128)} copy(f32[1,2,2,128]{3,2,1,0:T(2,128)} %bitcast.6) | data formatting | bytes 4096
  117.6 1.2 %copy.12 = f32[1,2,2,128]{3,2,1,0:T(2,128)} copy(f32[1,2,2,128]{3,2,1,0:T(2,128)} %bitcast.5) | data formatting | bytes 4096

commit v6 on v5

--- a/solution.py
+++ b/solution.py
@@ -18,7 +18,7 @@
 QUAD = 8
 SIDE = 33
 CHUNKS = 4
-DETOUR = 3
+DETOUR = 4
 MESH = pl.DeviceIdType.MESH
 
 spring_weight = 1.0
@@ -79,7 +79,7 @@
     return three(jnp.concatenate([ar * br + ai * bi, ar * bi - ai * br], 1), 1)
 
 
-def flow_chunk(loads, base, down, across, back, up, u_high, u_low, u_edge, g_edge, stat, between):
+def flow_chunk(loads, base, down, across, back, up, u_high, u_low, u_edge, g_edge, stat):
     for s in range(2):
         for tile in range(0, TILES + 1, 2):
             n = min(2, TILES + 1 - tile)
@@ -111,7 +111,6 @@
     real_rows = jnp.concatenate([across[i * 256 : i * 256 + 128] for i in range(3)], 0)
     spec = dot(three(jnp.concatenate(blocks, 0), 1), real_rows)
     g_edge[...] = dot(cross(spec, count), back[...])[:, :128]
-    between()
 
     def some(i, carry):
         left = []
@@ -310,7 +309,7 @@
 
     def step(i):
         apart = jnp.logical_or(lower, upper)
-        half = jnp.where(apart, lax.rem(i // CHUNKS + jnp.where(upper, 1, 0), 2), lax.rem(i, 2))
+        half = lax.rem(jnp.where(apart, i // CHUNKS, i) + jnp.where(jnp.logical_or(upper, last), 1, 0), 2)
         return half, CHUNKS - 1 - jnp.where(apart, lax.rem(i, CHUNKS), i // 2)
 
     @pl.when(gives(0))
@@ -382,12 +381,9 @@
     def one(i, carry):
         half, c = step(i)
 
-        def advance():
-            @pl.when(i + 1 < 2 * CHUNKS)
-            def _():
-                arrive(*step(i + 1))
-
-        pl.when(jnp.logical_not(works(half)))(advance)
+        @pl.when(i + 1 < 2 * CHUNKS)
+        def _():
+            arrive(*step(i + 1))
 
         @pl.when(works(half))
         def _():
@@ -404,7 +400,7 @@
                 return load
 
             base = half * PATCH + c * TILES * 2
-            flow_chunk([loader(0), loader(1)], base, down, across, back, up, u_high, u_low, u_edge, g_edge, stat, advance)
+            flow_chunk([loader(0), loader(1)], base, down, across, back, up, u_high, u_low, u_edge, g_edge, stat)
 
         return carry
 

time: 120 us -> 113 us (0.942)
  Pallas kernels: 116 us -> 108 us
    pallas_call x1, Pallas kernels: 29.9 us -> 20.4 us  [relaxed(): pl.pallas_call(relax_kernel, out_shape=(shape, shape), in_specs=[vmem] *...]
    pallas_call x1, Pallas kernels: 85.8 us -> 87.5 us  [flow_of(): pl.pallas_call(flow_kernel, out_shape=jax.ShapeDtypeStruct((2, 2, 2, 128)...]
where the time goes in v6:
time: 113 us; the launch traced here: 111 us
  Pallas kernels  108 us (96%)
  local copies, waits for them, and re-layouts  2.48 us (2%)
    pallas_call x1, Pallas kernels, flow_of(): pl.pallas_call(flow_kernel, out_shape=jax.ShapeDtypeStruct((2, 2, 2, 128)...  87.5 us
    pallas_call x1, Pallas kernels, relaxed(): pl.pallas_call(relax_kernel, out_shape=(shape, shape), in_specs=[vmem] *...  20.4 us
    unnamed x2, local copies, waits for them, and re-layouts  2.48 us

profile of v6, /device:TPU:3, one launch (start us, length us, event | category | flops | bytes accessed | tf_op | source)
XLA Modules:
  0.0 111.1 jit_solution(646417691598342908)
XLA Ops:
  0.6 87.5 %shard_map.86.pieces = f32[2,2,2,128]{3,2,1,0:T(2,128)} custom-call(f32[128,8192]{1,0:T(8,128)} %bitcast.4, bf16[144,384]{1,0:T(8,128)(2,1)} %constant.8.clone.down, bf16[768,256]{1,0:T(8,128)(2,1)} %constant.9.clone.across, bf16[768,256]{1,0:T(8,128)(2,1)} %constant.10.clone.back, bf16[128,384]{1,0:T(8,128)(2,1)} %constant.11.clone.up), custom_call_target="tpu_custom_call" | custom-call | tf_op jit(solution)/shard_map/pallas_call | solution.py:451
  88.1 20.4 %shard_map.87 = (f32[2,2,128]{2,1,0:T(2,128)}, f32[2,2,128]{2,1,0:T(2,128)}) custom-call(f32[2,2,2,128]{3,2,1,0:T(2,128)} %shard_map.86.pieces, s32[2,128]{1,0:T(2,128)} %bitcast.7, f32[2,2,128]{2,1,0:T(2,128)} %carried.1), custom_call_target="tpu_custom_call" | custom-call | tf_op jit(solution)/shard_map/pallas_call | solution.py:590
  108.6 1.2 %copy.11 = f32[1,2,2,128]{3,2,1,0:T(2,128)} copy(f32[1,2,2,128]{3,2,1,0:T(2,128)} %bitcast.6) | data formatting | bytes 4096
  109.8 1.2 %copy.12 = f32[1,2,2,128]{3,2,1,0:T(2,128)} copy(f32[1,2,2,128]{3,2,1,0:T(2,128)} %bitcast.5) | data formatting | bytes 4096

commit v7 on v6

--- a/solution.py
+++ b/solution.py
@@ -467,7 +467,7 @@
     )(x, *(jnp.asarray(t) for t in tables()))
 
 
-def relax_kernel(pieces, masks, carried, flow_out, aligned_out, mine, blocks, result, sec_send, sec_recv, tile_send, tile_recv):
+def relax_kernel(pieces, masks, carried, out, mine, blocks, result, sec_send, sec_recv, tile_send, tile_recv):
     sec, tile = lax.axis_index("sec"), lax.axis_index("tile")
     secs, tiles = lax.axis_size("sec"), lax.axis_size("tile")
     barrier = pltpu.get_barrier_semaphore()
@@ -574,8 +574,8 @@
             result[s, k] = flow[s][k]
             result[s, 2 + k] = aligned[s][k]
     for k in range(2):
-        flow_out[k] = result[sec, k][3:5]
-        aligned_out[k] = result[sec, 2 + k][3:5]
+        out[0, k] = result[sec, k][3:5]
+        out[1, k] = result[sec, 2 + k][3:5]
     for k in range(1, secs):
         to_sec(k, sec).wait_send()
     for copy in copies:
@@ -586,12 +586,11 @@
     vmem = pl.BlockSpec(memory_space=pltpu.VMEM)
     dma = pltpu.SemaphoreType.DMA
     secs = lax.axis_size("sec")
-    shape = jax.ShapeDtypeStruct((2, 2, 128), f32)
     return pl.pallas_call(
         relax_kernel,
-        out_shape=(shape, shape),
+        out_shape=jax.ShapeDtypeStruct((2, 2, 2, 128), f32),
         in_specs=[vmem] * 3,
-        out_specs=(vmem, vmem),
+        out_specs=vmem,
         scratch_shapes=[
             pltpu.VMEM((secs, 16, 128), f32),
             pltpu.VMEM((5, secs, 8, 128), f32),
@@ -606,8 +605,8 @@
 
 
 def shards(sections, masks, carried):
-    flow, aligned = relaxed(flow_of(sections[0]), masks[0], carried)
-    return flow[None], aligned[None]
+    both = relaxed(flow_of(sections[0]), masks[0], carried)
+    return both[0:1], both[1:2]
 
 
 def solution(mesh):

time: 113 us -> 112 us (level)
  local copies, waits for them, and re-layouts: 2.48 us -> 1.26 us
    unnamed x2 -> x0, local copies, waits for them, and re-layouts: 2.48 us -> none
    slice x0 -> x1, local copies, waits for them, and re-layouts: none -> 1.26 us  [shards(): return (both[0:1], both[1:2])]
where the time goes in v7:
time: 112 us; the launch traced here: 110 us
  Pallas kernels  108 us (96%)
  local copies, waits for them, and re-layouts  1.26 us (1%)
    pallas_call x1, Pallas kernels, flow_of(): pl.pallas_call(flow_kernel, out_shape=jax.ShapeDtypeStruct((2, 2, 2, 128)...  87.5 us
    pallas_call x1, Pallas kernels, relaxed(): pl.pallas_call(relax_kernel, out_shape=jax.ShapeDtypeStruct((2, 2, 2, 128...  20.5 us

profile of v7, /device:TPU:3, one launch (start us, length us, event | category | flops | bytes accessed | tf_op | source)
XLA Modules:
  0.0 109.9 jit_solution(14607757293698950029)
XLA Ops:
  0.6 87.5 %shard_map.86.pieces = f32[2,2,2,128]{3,2,1,0:T(2,128)} custom-call(f32[128,8192]{1,0:T(8,128)} %bitcast.2, bf16[144,384]{1,0:T(8,128)(2,1)} %constant.8.clone.down, bf16[768,256]{1,0:T(8,128)(2,1)} %constant.9.clone.across, bf16[768,256]{1,0:T(8,128)(2,1)} %constant.10.clone.back, bf16[128,384]{1,0:T(8,128)(2,1)} %constant.11.clone.up), custom_call_target="tpu_custom_call" | custom-call | tf_op jit(solution)/shard_map/pallas_call | solution.py:451
  88.1 20.5 %shard_map.87 = f32[2,2,2,128]{3,2,1,0:T(2,128)} custom-call(f32[2,2,2,128]{3,2,1,0:T(2,128)} %shard_map.86.pieces, s32[2,128]{1,0:T(2,128)} %bitcast.3, f32[2,2,128]{2,1,0:T(2,128)} %carried.1), custom_call_target="tpu_custom_call" | custom-call | tf_op jit(solution)/shard_map/pallas_call | solution.py:589
  108.6 1.3 %fusion = (f32[1,2,2,128]{3,2,1,0:T(2,128)}, f32[1,2,2,128]{3,2,1,0:T(2,128)}) fusion(f32[2,2,2,128]{3,2,1,0:T(2,128)} %shard_map.87), kind=kLoop, calls=%fused_computation | loop fusion | bytes 8192 | tf_op jit(solution)/shard_map/slice | solution.py:609
